TPU v7x, 512 devices: a whole 4x4x16 slice. The times are simulated.
512 devices in a mesh: rep: 8 (over z_lo, core), fsdp: 64 (over z_hi, x, y).
Axes of the slice: x: 4, y: 4, z: 16 (z_hi: 4, z_lo: 4; z = z_hi * 4 + z_lo), core: 2. Of those that a mesh axis runs over, the one named last changes fastest.
Arguments:
- gu_pseudo: bfloat16 [8, 64, 2, 4, 28672], P('rep', 'fsdp'), may hold values from -6 to 6
- gu_master: float32 [2, 4, 28672], P(None, None, 'fsdp'), may hold values from -6 to 6
- gu_moment: float32 [2, 4, 28672], P(None, None, 'fsdp'), may hold values from -6 to 6
- down_pseudo: bfloat16 [8, 64, 64, 8192], P('rep', 'fsdp'), may hold values from -6 to 6
- down_master: float32 [64, 8192], P(None, 'fsdp'), may hold values from -6 to 6
- down_moment: float32 [64, 8192], P(None, 'fsdp'), may hold values from -6 to 6
Outputs:
- gu_params: bfloat16 [2, 4, 28672], replicated
- down_params: bfloat16 [64, 8192], replicated
- gu_master_new: float32 [2, 4, 28672], P(None, None, 'fsdp')
- down_master_new: float32 [64, 8192], P(None, 'fsdp')
- gu_moment_new: float32 [2, 4, 28672], P(None, None, 'fsdp')
- down_moment_new: float32 [64, 8192], P(None, 'fsdp')
- gu_scale: float32 [2, 4, 448], P(None, None, 'fsdp')
- down_scale: float32 [64, 128], P(None, 'fsdp')
All inputs are finite; a program needn't handle non-finite values. Where the computation divides by a largest or mean magnitude, that divisor is 1e-20 or more.
Results may differ from a plain program's by a relative error of at most 0.015.
Values may be sent and summed in bfloat16 or wider, within the bound.
A program may use at most 128 MiB of HBM per device.

v0:
```python
import jax
import jax.numpy as jnp
from jax import lax
from jax.sharding import PartitionSpec as P

BLOCK = 64


def finish(partial_value, master, moment):
    rows, cols = partial_value.shape
    blocks = partial_value.reshape(rows, cols // BLOCK, BLOCK)
    local_max = jnp.max(jnp.abs(blocks), axis=-1)
    scale = lax.pmax(local_max, "rep") + 1e-06
    coded = (blocks / scale[..., None]).astype(jnp.bfloat16).astype(jnp.float32)
    total = lax.psum(coded.astype(jnp.bfloat16), "rep").astype(jnp.float32)
    delta = (scale[..., None] * total).reshape(rows, cols) / lax.axis_size("rep")
    moment_new = 0.9 * moment + delta
    master_new = master - 0.7 * (delta + 0.9 * moment_new)
    params = lax.all_gather(master_new.astype(jnp.bfloat16), "fsdp", axis=1, tiled=True)
    return (params, master_new, moment_new, scale)


def per_device(gu_pseudo, gu_master, gu_moment, down_pseudo, down_master, down_moment):
    grows = gu_master.shape[1]
    gu_terms = gu_pseudo[0, 0].reshape(2 * grows, gu_pseudo.shape[4])
    down_terms = down_pseudo[0, 0]
    gu_shard_master = gu_master.reshape(2 * grows, gu_master.shape[2])
    gu_shard_moment = gu_moment.reshape(2 * grows, gu_moment.shape[2])
    gu_part, down_part = (
        lax.psum_scatter(gu_terms.astype(jnp.float32), "fsdp", scatter_dimension=1, tiled=True),
        lax.psum_scatter(down_terms.astype(jnp.float32), "fsdp", scatter_dimension=1, tiled=True),
    )
    gu_out = finish(gu_part, gu_shard_master, gu_shard_moment)
    down_out = finish(down_part, down_master, down_moment)
    gu_params = gu_out[0].reshape(2, grows, gu_out[0].shape[1])
    gu_master_new = gu_out[1].reshape(gu_master.shape)
    gu_moment_new = gu_out[2].reshape(gu_moment.shape)
    gu_scale = gu_out[3].reshape(2, grows, gu_out[3].shape[1])
    return (
        gu_params,
        down_out[0],
        gu_master_new,
        down_out[1],
        gu_moment_new,
        down_out[2],
        gu_scale,
        down_out[3],
    )


def solution(mesh):
    in_specs = (
        P("rep", "fsdp", None, None, None),
        P(None, None, "fsdp"),
        P(None, None, "fsdp"),
        P("rep", "fsdp", None, None),
        P(None, "fsdp"),
        P(None, "fsdp"),
    )
    out_specs = (
        P(),
        P(),
        P(None, None, "fsdp"),
        P(None, "fsdp"),
        P(None, None, "fsdp"),
        P(None, "fsdp"),
        P(None, None, "fsdp"),
        P(None, "fsdp"),
    )
    return jax.shard_map(
        per_device, mesh=mesh, in_specs=in_specs, out_specs=out_specs, check_vma=False
    )
```

profile of v0, /device:TPU:1, one launch (start us, length us, event | category | flops | bytes accessed | tf_op | source)
XLA Modules:
  0.0 1459.2 jit_solution(13924592738567931397)
XLA Ops:
  7.2 1.1 reshape.57
  8.3 8.2 copy.19
  16.6 1.1 copy-done
  17.7 1.5 bitcast_convert_fusion
  19.3 720.8 %reduce-scatter.7.cloned.1.call-done = f32[448,8]{1,0:T(8,128)} async-done(((f32[28672,8]{1,0:T(8,128)}), f32[448,8]{1,0:T(8,128)}) %reduce-scatter.7.cloned.1.call-update) | async-done | bytes 14352
  740.1 1.1 copy.21
  741.2 0.1 abs_reduce_fusion.1
  741.2 403.1 %reduce-scatter.5.cloned.1.call-done = f32[64,128]{1,0:T(8,128)} async-done(((f32[64,8192]{1,0:T(8,128)}), f32[64,128]{1,0:T(8,128)}) %reduce-scatter.5.cloned.1.call-update) | async-done | bytes 32784 | tf_op jit(solution)/shard_map/reduce_scatter | solution.py:31
  1144.3 0.9 reshape.55
  1145.2 0.1 abs_reduce_fusion
  1145.4 74.6 %all-reduce = (f32[8,7]{1,0:T(8,128)S(1)}, f32[64,2]{1,0:T(8,128)S(1)}) all-reduce(f32[8,7]{1,0:T(8,128)S(1)} %abs_reduce_fusion.1, f32[64,2]{1,0:T(8,128)S(1)} %abs_reduce_fusion), channel_id=1, replica_groups=mesh['rep'=8,'fsdp'=64] {'rep'}, use_global_device_ids=true, to_apply=%region_2.0 | all-reduce | flops 184 | bytes 1472 | tf_op jit(solution)/shard_map/pmax | solution.py:13
  1219.9 0.1 divide_convert_fusion
  1220.1 0.1 divide_convert_fusion.1
  1220.2 26.4 %all-reduce.1 = (bf16[8,7,64]{2,1,0:T(8,128)(2,1)S(1)}, bf16[64,2,64]{2,1,0:T(2,128)(2,1)S(1)}) all-reduce(bf16[8,7,64]{2,1,0:T(8,128)(2,1)S(1)} %divide_convert_fusion.1, bf16[64,2,64]{2,1,0:T(2,128)(2,1)S(1)} %divide_convert_fusion), channel_id=1, replica_groups=mesh['rep'=8,'fsdp'=64] {'rep'}, use_global_device_ids=true, to_apply=%region_3.0 | all-reduce | flops 11776 | bytes 47104 | tf_op jit(solution)/shard_map/psum | solution.py:15
  1246.5 0.1 multiply_multiply_fusion
  1246.7 0.1 div.37
  1246.8 0.6 fusion.3
  1247.7 0.6 copy.18
  1248.3 0.6 multiply_subtract_fusion.1
  1249.0 199.7 %all-gather = bf16[64,448,8]{1,2,0:T(8,128)(2,1)S(1)} all-gather(bf16[1,448,8]{1,2,0:T(8,128)(2,1)S(1)} %fusion), channel_id=1, replica_groups=mesh['rep'=8,'fsdp'=64] {'fsdp'}, dimensions={0}, use_global_device_ids=true | all-gather | bytes 465920 | tf_op jit(solution)/shard_map/all_gather | solution.py:19
  1448.7 0.2 copy.17
  1448.9 0.6 reshape.60
  1449.5 0.9 reshape.54
  1450.4 2.3 copy.23
  (26 shorter events, 0.5 us)
Async XLA Ops:
  7.2 732.9 %reduce-scatter.7.cloned.1.call-start = ((), (), s32[]{:S(2)}) async-start(), calls=%async_computation.4 | async-start | bytes 14909440
  16.5 1.2 copy-start
  16.5 1127.8 %reduce-scatter.5.cloned.1.call-start = ((), (), s32[]{:S(2)}) async-start(), calls=%async_computation.2 | async-start | bytes 2129920 | tf_op jit(solution)/shard_map/reduce_scatter | solution.py:31
  19.2 1227.6 %copy-start.3 = (f32[64,128]{1,0:T(8,128)S(1)}, f32[64,128]{1,0:T(8,128)}, u32[]{:S(2)}) copy-start(f32[64,128]{1,0:T(8,128)} %param.10) | copy-start | bytes 98308
  19.2 1227.6 %copy-start.4 = (f32[64,128]{1,0:T(8,128)S(1)}, f32[64,128]{1,0:T(8,128)}, u32[]{:S(2)}) copy-start(f32[64,128]{1,0:T(8,128)} %param.11) | copy-start | bytes 98308
  19.2 1228.2 %copy-start.1 = (f32[2,4,448]{2,1,0:T(4,128)S(1)}, f32[2,4,448]{2,1,0:T(4,128)}, u32[]{:S(2)}) copy-start(f32[2,4,448]{2,1,0:T(4,128)} %param.7) | copy-start | bytes 43012
  19.2 1229.1 %copy-start.5 = (f32[2,4,448]{2,1,0:T(4,128)S(1)}, f32[2,4,448]{2,1,0:T(4,128)}, u32[]{:S(2)}) copy-start(f32[2,4,448]{2,1,0:T(4,128)} %param.8) | copy-start | bytes 43012
  19.2 1431.2 %all-gather.3.cloned.1.call-start = ((), (), s32[]{:S(2)}) async-start(), calls=%async_computation.3 | async-start | bytes 1064960 | tf_op jit(solution)/shard_map/all_gather | solution.py:19
  1220.1 230.3 %copy-start.2 = (f32[8,7]{1,0:T(8,128)}, f32[8,7]{1,0:T(8,128)S(1)}, u32[]{:S(2)}) copy-start(f32[8,7]{1,0:T(8,128)S(1)} %broadcast_add_fusion.1) | copy-start | bytes 676
Sparse Core Ops, SparseCore 0:
  16.7 723.4 reduce-scatter.6
  742.9 401.4 reduce-scatter.4
  1247.6 106.9 all-gather.2
where the time goes:
time: 1480 us; the launch traced here: 1460 us
  waiting for transfers between devices  1120 us (76%)
  blocking collectives  301 us (20%)
  local copies, waits for them, and re-layouts  17.2 us (1%)
    unnamed x4, waiting for transfers between devices  721 us
    reduce_scatter x1, waiting for transfers between devices, per_device(): lax.psum_scatter(down_terms.astype(jnp.float32), 'fsdp', scatter_dimensio...  403 us
    all_gather x1, blocking collectives, finish(): lax.all_gather(master_new.astype(jnp.bfloat16), 'fsdp', axis=1, tiled=True)  200 us
    pmax x1, blocking collectives, finish(): scale = lax.pmax(local_max, 'rep') + 1e-06  74.6 us
  transfers between devices with their start and end apart: 3, of which 2 were waited for; matrix products, arithmetic and copies ran while one was open for 0% of the time, Pallas kernels for 0%

commit v1 on v0

v1 whole, which is shorter than its diff:
```python
import functools

import jax
import jax.numpy as jnp
from jax import lax
from jax.experimental import pallas as pl
from jax.experimental.pallas import tpu as pltpu
from jax.sharding import PartitionSpec as P

NX = 4
NY = 4
ZH = 4
ZL = 4
LANES = 128
HALF = 64
GUCOLS = 448
TILES = 6
BF = jnp.bfloat16
F32 = jnp.float32

S1, S2, S3, SD, SG0, SG1, SG2, SC = 0, 2, 4, 5, 6, 7, 9, 11
NSEM = 13


def kernel(
    gu_ref, gm_ref, gmo_ref, dn_ref, dm_ref, dmo_ref,
    gu_out, dn_out, gm_out, dm_out, gmo_out, dmo_out, gs_out, ds_out,
    S, R1, PS, R2, Q, R3, D, G, M, MO, send, recv,
):
    rep = lax.axis_index("rep")
    fsdp = lax.axis_index("fsdp")
    zl, core = rep // 2, rep % 2
    zh, x, y = fsdp // (NX * NY), (fsdp // NY) % NX, fsdp % NY
    z = zh * ZL + zl
    along = ((x, y), (y, x))

    def fs(zh_, x_, y_):
        return (zh_ * NX + x_) * NY + y_

    def first_peer(h, d):
        return fs(zh, d, y) if h == 0 else fs(zh, x, d)

    def second_peer(h, d):
        return fs(zh, x, d) if h == 0 else fs(zh, d, y)

    def remote(src, dst, sem, rep_, fsdp_):
        return pltpu.make_async_remote_copy(
            src_ref=src, dst_ref=dst, send_sem=send.at[sem], recv_sem=recv.at[sem],
            device_id={"rep": rep_, "fsdp": fsdp_}, device_id_type=pl.DeviceIdType.MESH,
        )

    def wait_bytes(ref, sem):
        pltpu.make_async_copy(ref, ref, sem).wait()

    barrier = pltpu.get_barrier_semaphore()

    def greet(rep_, fsdp_):
        pl.semaphore_signal(
            barrier, inc=1, device_id={"rep": rep_, "fsdp": fsdp_},
            device_id_type=pl.DeviceIdType.MESH,
        )

    for d in range(1, 4):
        greet(rep, fs(zh, (x + d) % 4, y))
        greet(rep, fs(zh, x, (y + d) % 4))

    def greet_line(k, carry):
        other = (z * 2 + core + k) % 32
        oz = other // 2
        greet((oz % ZL) * 2 + other % 2, fs(oz // ZL, x, y))
        return carry

    lax.fori_loop(1, 32, greet_line, 0)

    lane = lax.broadcasted_iota(jnp.int32, (8, 512), 1)
    for zh_ in range(ZH):
        h, z2 = zh_ // 2, zh_ % 2
        for x_ in range(NX):
            for y_ in range(NY):
                d1, d2 = (x_, y_) if h == 0 else (y_, x_)
                col = ((zh_ * NX + x_) * NY + y_) * LANES
                S[h, d1, d2, z2, 0:64, :] = dn_ref[0, 0, :, col : col + LANES]
            for yp in range(NY // 2):
                col = ((zh_ * NX + x_) * NY + 2 * yp) * GUCOLS
                both = jnp.concatenate(
                    [gu_ref[0, 0, g, :, col : col + 2 * GUCOLS].astype(F32) for g in range(2)], axis=0
                )
                odd = pltpu.roll(both[:, 384:896], 512 - HALF, 1)
                for o, part in enumerate((both[:, 0:512], odd)):
                    part = jnp.where(lane < GUCOLS, part, 0.0)
                    y_ = 2 * yp + o
                    d1, d2 = (x_, y_) if h == 0 else (y_, x_)
                    for t in range(2):
                        two = jnp.concatenate(
                            [part[:, 256 * t : 256 * t + 128], part[:, 256 * t + 128 : 256 * t + 256]], axis=0
                        )
                        S[h, d1, d2, z2, 64 + 16 * t : 80 + 16 * t, :] = two.astype(BF)
    for g_ref, d_ref, out in ((gm_ref, dm_ref, M), (gmo_ref, dmo_ref, MO)):
        for j in range(4):
            out[j] = d_ref[16 * j : 16 * j + 16, :]
        for g in range(2):
            for t in range(4):
                row = 8 * (t % 2) + 4 * g
                if t < 3:
                    out[4 + t // 2, row : row + 4, :] = g_ref[g, :, 128 * t : 128 * t + 128]
                else:
                    out[5, row : row + 4, :] = jnp.concatenate(
                        [g_ref[g, :, 384:448], jnp.zeros((4, HALF), F32)], axis=1
                    )

    pl.semaphore_wait(barrier, 37)

    for d in range(1, 4):
        for h in range(2):
            dest = (along[h][0] + d) % 4
            remote(S.at[h, dest], R1.at[h, d - 1], S1 + h, rep, first_peer(h, dest)).start()
    for h in range(2):
        mine, other = along[h]
        wait_bytes(R1.at[h], recv.at[S1 + h])
        for d in (1, 2, 3, 0):
            dest = (other + d) % 4
            acc = S[h, mine, dest].astype(F32)
            for i in range(3):
                acc = acc + R1[h, i, dest].astype(F32)
            PS[h, dest] = acc.astype(BF)
            if d:
                remote(PS.at[h, dest], R2.at[h, d - 1], S2 + h, rep, second_peer(h, dest)).start()
    for h in range(2):
        _, other = along[h]
        wait_bytes(R2.at[h], recv.at[S2 + h])
        acc = PS[h, other].astype(F32)
        for i in range(3):
            acc = acc + R2[h, i].astype(F32)
        Q[2 * h : 2 * h + 2] = acc.astype(BF).reshape(2, TILES, 16, LANES)

    for dz in range(4):
        to = (zh + dz) % 4
        for j in range(TILES):
            copy = remote(Q.at[to, j], R3.at[zh * 8 + rep], S3, j, fs(to, x, y))
            if dz:
                copy.start()
            else:
                pl.when(rep != j)(copy.start)

    @pl.when(rep < TILES)
    def _():
        R3[zh * 8 + rep] = Q[zh, rep]
        wait_bytes(R3.at[pl.ds(0, 31)], recv.at[S3])
        largest = jnp.zeros((16, LANES), F32)
        total = jnp.zeros((16, LANES), F32)
        for r in range(8):
            part = R3[r].astype(F32)
            for k in range(1, 4):
                part = part + R3[8 * k + r].astype(F32)
            largest = jnp.maximum(largest, jnp.abs(part))
            total = total + part
        low = lax.broadcasted_iota(jnp.int32, (16, LANES), 1) < HALF
        low_max = jnp.max(jnp.where(low, largest, 0.0), axis=1, keepdims=True)
        high_max = jnp.max(jnp.where(low, 0.0, largest), axis=1, keepdims=True)
        delta = total / 8
        D[rep, 0] = delta
        D[rep, 1] = jnp.where(low, low_max, high_max) + 1e-6
        moment = 0.9 * MO[rep] + delta
        master = M[rep] - 0.7 * (delta + 0.9 * moment)
        hh = zh // 2
        d1 = jnp.where(hh == 0, x, y)
        d2 = jnp.where(hh == 0, y, x)
        mine = G.at[core, hh, d1, d2, zh % 2, zl]
        mine[...] = master.astype(BF)

        def spread(k, carry):
            oz = (z + k) % 16
            remote(mine, mine, SG0, (oz % ZL) * 2 + core, fs(oz // ZL, x, y)).start()
            return carry

        lax.fori_loop(1, 16, spread, 0)
        for k in range(1, 8):
            remote(D.at[rep], D.at[rep], SD, (rep + k) % 8, fsdp).start()
        wait_bytes(R3.at[pl.ds(0, 11)], recv.at[SG0])

    @pl.when(rep >= TILES)
    def _():
        wait_bytes(R3.at[pl.ds(0, 12)], recv.at[SG0])

    for h in range(2):
        mine, other = along[h]
        for d in range(1, 4):
            dest = (other + d) % 4
            block = G.at[core, h, mine, other]
            remote(block, block, SG1 + h, rep, second_peer(h, dest)).start()

    @pl.when(rep < TILES)
    def _():
        wait_bytes(D.at[pl.ds(0, 5)], recv.at[SD])

    @pl.when(rep >= TILES)
    def _():
        wait_bytes(D, recv.at[SD])

    low = lax.broadcasted_iota(jnp.int32, (16, LANES), 1)
    moments, masters, scales = [], [], []
    for j in range(TILES):
        moment = 0.9 * MO[j] + D[j, 0]
        moments.append(moment)
        masters.append(M[j] - 0.7 * (D[j, 0] + 0.9 * moment))
        scales.append(D[j, 1])
    for tiles, d_out, g_out in ((moments, dmo_out, gmo_out), (masters, dm_out, gm_out)):
        for j in range(4):
            d_out[16 * j : 16 * j + 16, :] = tiles[j]
        for g in range(2):
            for t in range(4):
                row = 8 * (t % 2) + 4 * g
                width = 128 if t < 3 else 64
                g_out[g, :, 128 * t : 128 * t + width] = tiles[4 + t // 2][row : row + 4, :width]
    for j in range(4):
        pair = jnp.where(low == 0, scales[j], pltpu.roll(scales[j], HALF, 1))
        ds_out[16 * j : 16 * j + 16, :] = pair[:, 0:2]
    lane8 = lax.broadcasted_iota(jnp.int32, (8, LANES), 1)
    acc = jnp.zeros((8, LANES), F32)
    for t in range(4):
        tile = scales[4 + t // 2][8 * (t % 2) : 8 * (t % 2) + 8]
        acc = jnp.where(lane8 == 2 * t, tile, acc)
        acc = jnp.where(lane8 == 2 * t + 1, pltpu.roll(tile, HALF, 1), acc)
    for g in range(2):
        gs_out[g, :, :] = acc[4 * g : 4 * g + 4, 0:7]

    sibling = zl * 2 + (1 - core)
    for h in range(2):
        mine, other = along[h]
        wait_bytes(G.at[core, h, mine, pl.ds(0, 3)], recv.at[SG1 + h])
        block = G.at[core, h, mine]
        for d in range(1, 4):
            dest = (mine + d) % 4
            remote(block, block, SG2 + h, rep, first_peer(h, dest)).start()
        remote(block, block, SC + h, sibling, fsdp).start()
    for h in range(2):
        mine, other = along[h]
        wait_bytes(G.at[core, h, pl.ds(0, 3)], recv.at[SG2 + h])
        for d in range(1, 4):
            block = G.at[core, h, (mine + d) % 4]
            remote(block, block, SC + h, sibling, fsdp).start()
    for h in range(2):
        wait_bytes(G.at[1 - core, h], recv.at[SC + h])
        for z2 in range(2):
            zh_ = 2 * h + z2
            for x_ in range(NX):
                gu_tiles = []
                for y_ in range(NY):
                    d1, d2 = (x_, y_) if h == 0 else (y_, x_)
                    col = ((zh_ * NX + x_) * NY + y_) * LANES
                    for j in range(4):
                        dn_out[16 * j : 16 * j + 16, col : col + LANES] = G[j % 2, h, d1, d2, z2, j // 2]
                    wide = []
                    for c in range(2):
                        tile = G[c, h, d1, d2, z2, 2].astype(F32)
                        wide += [tile[0:8], tile[8:16]]
                    gu_tiles.append(wide)
                for yp in range(NY // 2):
                    even, odd = gu_tiles[2 * yp], gu_tiles[2 * yp + 1]
                    odd = pltpu.roll(jnp.concatenate(odd, axis=1), HALF, 1)
                    joined = jnp.where(lane8 < HALF, even[3], odd[:, 0:128])
                    full = jnp.concatenate(even[:3] + [joined, odd[:, 128:512]], axis=1)
                    col = ((zh_ * NX + x_) * NY + 2 * yp) * GUCOLS
                    for g in range(2):
                        gu_out[g, :, col : col + 2 * GUCOLS] = full[4 * g : 4 * g + 4].astype(BF)

    for h in range(2):
        mine, other = along[h]
        wait_bytes(S.at[h, pl.ds(0, 3)], send.at[S1 + h])
        wait_bytes(PS.at[h, pl.ds(0, 3)], send.at[S2 + h])
        wait_bytes(G.at[core, h, mine, pl.ds(0, 3)], send.at[SG1 + h])
        wait_bytes(G.at[core, h, pl.ds(0, 3)], send.at[SG2 + h])
        wait_bytes(G.at[core, h], send.at[SC + h])

    @pl.when(rep < TILES)
    def _():
        wait_bytes(R3.at[pl.ds(0, 23)], send.at[S3])
        wait_bytes(R3.at[pl.ds(0, 15)], send.at[SG0])
        wait_bytes(R3.at[pl.ds(0, 28)], send.at[SD])

    @pl.when(rep >= TILES)
    def _():
        wait_bytes(R3.at[pl.ds(0, 24)], send.at[S3])


def per_device(gu_pseudo, gu_master, gu_moment, down_pseudo, down_master, down_moment):
    full_gu = gu_pseudo.shape[2:]
    full_dn = down_pseudo.shape[2:]
    vmem = pl.BlockSpec(memory_space=pltpu.VMEM)
    return pl.pallas_call(
        kernel,
        out_shape=(
            jax.ShapeDtypeStruct(full_gu, BF),
            jax.ShapeDtypeStruct(full_dn, BF),
            jax.ShapeDtypeStruct(gu_master.shape, F32),
            jax.ShapeDtypeStruct(down_master.shape, F32),
            jax.ShapeDtypeStruct(gu_master.shape, F32),
            jax.ShapeDtypeStruct(down_master.shape, F32),
            jax.ShapeDtypeStruct(gu_master.shape[:2] + (7,), F32),
            jax.ShapeDtypeStruct((down_master.shape[0], 2), F32),
        ),
        in_specs=[vmem] * 6,
        out_specs=[vmem] * 8,
        scratch_shapes=[
            pltpu.VMEM((2, 4, 4, 2, 96, LANES), BF),
            pltpu.VMEM((2, 3, 4, 2, 96, LANES), BF),
            pltpu.VMEM((2, 4, 2, 96, LANES), BF),
            pltpu.VMEM((2, 3, 2, 96, LANES), BF),
            pltpu.VMEM((4, TILES, 16, LANES), BF),
            pltpu.VMEM((32, 16, LANES), BF),
            pltpu.VMEM((TILES, 2, 16, LANES), F32),
            pltpu.VMEM((2, 2, 4, 4, 2, 3, 16, LANES), BF),
            pltpu.VMEM((TILES, 16, LANES), F32),
            pltpu.VMEM((TILES, 16, LANES), F32),
            pltpu.SemaphoreType.DMA((NSEM,)),
            pltpu.SemaphoreType.DMA((NSEM,)),
        ],
        compiler_params=pltpu.CompilerParams(
            collective_id=0, has_side_effects=True, vmem_limit_bytes=32 * 1024 * 1024
        ),
    )(gu_pseudo, gu_master, gu_moment, down_pseudo, down_master, down_moment)


def solution(mesh):
    in_specs = (
        P("rep", "fsdp", None, None, None),
        P(None, None, "fsdp"),
        P(None, None, "fsdp"),
        P("rep", "fsdp", None, None),
        P(None, "fsdp"),
        P(None, "fsdp"),
    )
    out_specs = (
        P(),
        P(),
        P(None, None, "fsdp"),
        P(None, "fsdp"),
        P(None, None, "fsdp"),
        P(None, "fsdp"),
        P(None, None, "fsdp"),
        P(None, "fsdp"),
    )
    return jax.shard_map(
        per_device, mesh=mesh, in_specs=in_specs, out_specs=out_specs, check_vma=False
    )
```

time: 1480 us -> 76.4 us (0.05); the launches traced: 1460 us -> 76 us
  waiting for transfers between devices: 1120 us -> 0 us
  blocking collectives: 301 us -> 0 us
  Pallas kernels: 0 us -> 64.7 us
    unnamed x4 -> x0, waiting for transfers between devices: 721 us -> none
    reduce_scatter x1 -> x0, waiting for transfers between devices: 403 us -> none  [per_device(): lax.psum_scatter(down_terms.astype(jnp.float32), 'fsdp', scatter_dimensio...]
    all_gather x1 -> x0, blocking collectives: 200 us -> none  [finish(): lax.all_gather(master_new.astype(jnp.bfloat16), 'fsdp', axis=1, tiled=True)]
    pmax x1 -> x0, blocking collectives: 74.6 us -> none  [finish(): scale = lax.pmax(local_max, 'rep') + 1e-06]
    pallas_call x0 -> x1, Pallas kernels: none -> 64.7 us  [per_device(): pl.pallas_call(kernel, out_shape=(jax.ShapeDtypeStruct(full_gu, BF), jax....]
    psum x1 -> x0, blocking collectives: 26.4 us -> none  [finish(): total = lax.psum(coded.astype(jnp.bfloat16), 'rep').astype(jnp.float32)]
  transfers between devices with their start and end apart: 3 -> 0, of which waited for: 2 -> 0; matrix products, arithmetic and copies ran while one was open for 0% -> 0% of each run, Pallas kernels for 0% -> 0%
where the time goes in v1:
time: 76.4 us; the launch traced here: 76 us
  Pallas kernels  64.7 us (85%)
  local copies, waits for them, and re-layouts  10.6 us (14%)
    pallas_call x1, Pallas kernels, per_device(): pl.pallas_call(kernel, out_shape=(jax.ShapeDtypeStruct(full_gu, BF), jax....  64.7 us
    unnamed x19, local copies, waits for them, and re-layouts  9.95 us

profile of v1, /device:TPU:1, one launch (start us, length us, event | category | flops | bytes accessed | tf_op | source)
XLA Modules:
  0.0 76.0 jit_solution(14398718198584222033)
XLA Ops:
  0.6 0.0 copy-start
  0.6 1.2 %copy-done = bf16[1,1,64,8192]{3,2,1,0:T(8,128)(2,1)S(1)} copy-done((bf16[1,1,64,8192]{3,2,1,0:T(8,128)(2,1)S(1)}, bf16[1,1,64,8192]{3,2,1,0:T(8,128)(2,1)}, u32[]{:S(2)}) %copy-start) | copy-done | bytes 1048600
  1.9 0.0 copy-start.1
  1.9 1.0 %copy-done.1 = bf16[1,1,2,4,28672]{4,3,2,1,0:T(4,128)(2,1)S(1)} copy-done((bf16[1,1,2,4,28672]{4,3,2,1,0:T(4,128)(2,1)S(1)}, bf16[1,1,2,4,28672]{4,3,2,1,0:T(4,128)(2,1)}, u32[]{:S(2)}) %copy-start.1) | copy-done | bytes 458776
  2.9 0.0 copy-start.2
  2.9 0.8 copy-done.2
  3.6 0.0 copy-start.3
  3.6 0.8 copy-done.3
  4.4 0.0 copy-start.4
  4.4 0.7 copy-done.4
  5.1 0.0 copy-start.5
  5.1 0.7 copy-done.5
  5.8 64.7 %shard_map.125 = (bf16[2,4,28672]{2,1,0:T(4,128)(2,1)S(1)}, bf16[64,8192]{1,0:T(8,128)(2,1)S(1)}, f32[2,4,448]{2,1,0:T(4,128)S(1)}, f32[64,128]{1,0:T(8,128)S(1)...) custom-call(bf16[1,1,2,4,28672]{4,3,2,1,0:T(4,128)(2,1)S(1)} %copy-done.1, ...), custom_call_target="tpu_custom_call" | custom-call | tf_op jit(solution)/shard_map/pallas_call | solution.py:290
  70.6 0.6 copy.14
  71.2 0.8 %copy.22 = bf16[2,4,28672]{2,1,0:T(4,128)(2,1)} copy(bf16[2,4,28672]{2,1,0:T(4,128)(2,1)S(1)} %get-tuple-element.24) | data formatting | bytes 917504
  72.0 1.0 %copy.23 = bf16[64,8192]{1,0:T(8,128)(2,1)} copy(bf16[64,8192]{1,0:T(8,128)(2,1)S(1)} %get-tuple-element.25) | data formatting | bytes 2097152
  72.9 0.6 copy.24
  73.5 0.6 copy.25
  74.1 0.6 copy.26
  74.8 0.6 copy.27
  75.4 0.6 copy.28
Async XLA Ops:
  0.6 1.2 %copy-start = (bf16[1,1,64,8192]{3,2,1,0:T(8,128)(2,1)S(1)}, bf16[1,1,64,8192]{3,2,1,0:T(8,128)(2,1)}, u32[]{:S(2)}) copy-start(bf16[1,1,64,8192]{3,2,1,0:T(8,128)(2,1)} %dn_ref.1) | copy-start | bytes 3145732
  1.9 1.0 %copy-start.1 = (bf16[1,1,2,4,28672]{4,3,2,1,0:T(4,128)(2,1)S(1)}, bf16[1,1,2,4,28672]{4,3,2,1,0:T(4,128)(2,1)}, u32[]{:S(2)}) copy-start(bf16[1,1,2,4,28672]{4,3,2,1,0:T(4,128)(2,1)} %gu_ref.1) | copy-start | bytes 1376260
  2.9 0.8 copy-start.2
  3.6 0.8 copy-start.3
  4.4 0.7 copy-start.4
  5.1 0.7 copy-start.5

commit v2 on v1

v2 whole, which is shorter than its diff:
```python
import jax
import jax.numpy as jnp
from jax import lax
from jax.experimental import pallas as pl
from jax.experimental.pallas import tpu as pltpu
from jax.sharding import PartitionSpec as P

NX = 4
NY = 4
ZH = 4
ZL = 4
LANES = 128
HALF = 64
GUCOLS = 448
OWN = 3
BF = jnp.bfloat16
F32 = jnp.float32
MIB = 1024 * 1024

P1A, P1B, P2, Z3, Z0, SD, SDS, A1, A2A, A2B, A2R, SC = 0, 4, 6, 8, 9, 10, 11, 12, 14, 18, 22, 26
NSEM = 28


def kernel(
    gu_ref, gm_ref, gmo_ref, dn_ref, dm_ref, dmo_ref,
    gu_out, dn_out, gm_out, dm_out, gmo_out, dmo_out, gs_out, ds_out,
    gu_in, dn_in, gm_in, gmo_in, dm_in, dmo_in,
    S, RA, R1, PS, R2, Q, R3, D, G, M, MO, send, recv, local,
):
    rep = lax.axis_index("rep")
    fsdp = lax.axis_index("fsdp")
    zl, core = rep // 2, rep % 2
    zh, x, y = fsdp // (NX * NY), (fsdp // NY) % NX, fsdp % NY
    z = zh * ZL + zl
    along = ((x, y), (y, x))
    sibling = zl * 2 + (1 - core)

    def fs(zh_, x_, y_):
        return (zh_ * NX + x_) * NY + y_

    def first_peer(h, d):
        return fs(zh, d, y) if h == 0 else fs(zh, x, d)

    def second_peer(h, d):
        return fs(zh, x, d) if h == 0 else fs(zh, d, y)

    def remote(src, dst, out, sem, rep_, fsdp_):
        return pltpu.make_async_remote_copy(
            src_ref=src, dst_ref=dst, send_sem=send.at[out], recv_sem=recv.at[sem],
            device_id={"rep": rep_, "fsdp": fsdp_}, device_id_type=pl.DeviceIdType.MESH,
        )

    def wait_bytes(ref, sem):
        pltpu.make_async_copy(ref, ref, sem).wait()

    loads = [
        pltpu.make_async_copy(src, dst, local.at[i])
        for i, (src, dst) in enumerate(
            (
                (dn_ref, dn_in), (gu_ref, gu_in), (dm_ref, dm_in), (dmo_ref, dmo_in),
                (gm_ref, gm_in), (gmo_ref, gmo_in),
            )
        )
    ]
    for load in loads:
        load.start()
    barrier = pltpu.get_barrier_semaphore()

    def greet(rep_, fsdp_):
        pl.semaphore_signal(
            barrier, inc=1, device_id={"rep": rep_, "fsdp": fsdp_},
            device_id_type=pl.DeviceIdType.MESH,
        )

    def greet_line(k, carry):
        oz = (z + k) % 16
        greet((oz % ZL) * 2 + core, fs(oz // ZL, x, y))
        return carry

    lax.fori_loop(1, 16, greet_line, 0)
    greet(sibling, fsdp)
    for r in (rep, sibling):
        for d in range(1, 4):
            greet(r, fs(zh, (x + d) % 4, y))
            greet(r, fs(zh, x, (y + d) % 4))

    lane = lax.broadcasted_iota(jnp.int32, (8, 512), 1)
    lane8 = lax.broadcasted_iota(jnp.int32, (8, LANES), 1)
    loads[0].wait()
    for zh_ in range(ZH):
        h, z2 = zh_ // 2, zh_ % 2
        for x_ in range(NX):
            for y_ in range(NY):
                d1, d2 = (x_, y_) if h == 0 else (y_, x_)
                col = ((zh_ * NX + x_) * NY + y_) * LANES
                for c in range(2):
                    S[h, d1, d2, c, z2, 0:32, :] = dn_in[0, 0, 32 * c : 32 * c + 32, col : col + LANES]
    loads[1].wait()
    for zh_ in range(ZH):
        h, z2 = zh_ // 2, zh_ % 2
        for x_ in range(NX):
            for yp in range(NY // 2):
                col = ((zh_ * NX + x_) * NY + 2 * yp) * GUCOLS
                both = jnp.concatenate(
                    [gu_in[0, 0, g, :, col : col + 2 * GUCOLS].astype(F32) for g in range(2)], axis=0
                )
                odd = pltpu.roll(both[:, 384:896], 512 - HALF, 1)
                for o, part in enumerate((both[:, 0:512], odd)):
                    part = jnp.where(lane < GUCOLS, part, 0.0)
                    y_ = 2 * yp + o
                    d1, d2 = (x_, y_) if h == 0 else (y_, x_)
                    for c in range(2):
                        two = jnp.concatenate(
                            [part[:, 256 * c : 256 * c + 128], part[:, 256 * c + 128 : 256 * c + 256]], axis=0
                        )
                        S[h, d1, d2, c, z2, 32:48, :] = two.astype(BF)
    for load in loads[2:]:
        load.wait()
    for g_ref, d_ref, out in ((gm_in, dm_in, M), (gmo_in, dmo_in, MO)):
        for c in range(2):
            for k in range(2):
                row = 32 * c + 16 * k
                out[c, k] = d_ref[row : row + 16, :]
        for g in range(2):
            for t in range(4):
                row = 8 * (t % 2) + 4 * g
                if t < 3:
                    out[t // 2, 2, row : row + 4, :] = g_ref[g, :, 128 * t : 128 * t + 128]
                else:
                    out[1, 2, row : row + 4, :] = jnp.concatenate(
                        [g_ref[g, :, 384:448], jnp.zeros((4, HALF), F32)], axis=1
                    )

    pl.semaphore_wait(barrier, 28)

    def ways(h):
        mine = along[h][0]
        return (
            (0, (mine + 1) % 4, pl.ds(0, 2), pl.ds(2, 2)),
            (1, (mine + 3) % 4, pl.ds(2, 2), pl.ds(0, 2)),
        )

    for h in range(2):
        far = (along[h][0] + 2) % 4
        for w, near, on, _ in ways(h):
            remote(S.at[h, far, on], RA.at[h, w], P1B + h, P1A + 2 * h + w, rep, first_peer(h, near)).start()
    for h in range(2):
        for w, near, _, rest in ways(h):
            remote(S.at[h, near, rest], R1.at[h, w, rest], P1B + h, P1B + h, rep, first_peer(h, near)).start()
    for h in range(2):
        for w, near, on, _ in ways(h):
            wait_bytes(RA.at[h, w], recv.at[P1A + 2 * h + w])
            S[h, near, on] = (S[h, near, on].astype(F32) + RA[h, w].astype(F32)).astype(BF)
            remote(S.at[h, near, on], R1.at[h, w, on], P1B + h, P1B + h, rep, first_peer(h, near)).start()

    for h in range(2):
        mine, other = along[h]
        wait_bytes(R1.at[h], recv.at[P1B + h])
        for d in (2, 1, 3, 0):
            dest = (other + d) % 4
            acc = S[h, mine, dest].astype(F32) + R1[h, 0, dest].astype(F32) + R1[h, 1, dest].astype(F32)
            PS[h, dest] = acc.astype(BF)
            if d:
                to = second_peer(h, dest)
                slot = R2.at[h, 2 * (d - 1) + core]
                remote(PS.at[h, dest, core], slot, P2 + h, P2 + h, rep, to).start()
                remote(PS.at[h, dest, 1 - core], slot, P2 + h, P2 + h, sibling, to).start()
            else:
                remote(PS.at[h, dest, 1 - core], R2.at[h, 6 + core], P2 + h, P2 + h, sibling, fsdp).start()
                R2[h, 6 + core] = PS[h, dest, core]
    for h in range(2):
        wait_bytes(R2.at[h, pl.ds(0, 7)], recv.at[P2 + h])
        for c in range(2):
            acc = R2[h, c].astype(F32)
            for i in range(1, 4):
                acc = acc + R2[h, 2 * i + c].astype(F32)
            acc = acc.astype(BF).reshape(2, OWN, 16, LANES)
            for z2 in range(2):
                for k in range(OWN):
                    Q[2 * h + z2, k, c] = acc[z2, k]
        for z2 in range(2):
            for k in range(OWN):
                to = 2 * h + z2
                copy = remote(Q.at[to, k], R3.at[pl.ds(2 * z, 2)], Z3, Z3, 2 * k + core, fs(to, x, y))
                pl.when(jnp.logical_or(zh != to, zl != k))(copy.start)

    hh = zh // 2
    d1 = jnp.where(hh == 0, x, y)
    d2 = jnp.where(hh == 0, y, x)

    @pl.when(zl < OWN)
    def _():
        R3[pl.ds(2 * z, 2)] = Q[zh, zl]
        wait_bytes(R3.at[pl.ds(0, 30)], recv.at[Z3])
        largest = jnp.zeros((16, LANES), F32)
        total = jnp.zeros((16, LANES), F32)
        for r in range(8):
            part = R3[r].astype(F32)
            for k in range(1, 4):
                part = part + R3[8 * k + r].astype(F32)
            largest = jnp.maximum(largest, jnp.abs(part))
            total = total + part
        delta = total / 8
        moment = 0.9 * MO[core, zl] + delta
        master = M[core, zl] - 0.7 * (delta + 0.9 * moment)
        mine = G.at[core, hh, d1, d2, zh % 2, zl]
        mine[...] = master.astype(BF)

        def spread(k, carry):
            oz = (z + k) % 16
            remote(mine, mine, Z0, Z0, (oz % ZL) * 2 + core, fs(oz // ZL, x, y)).start()
            return carry

        lax.fori_loop(1, 16, spread, 0)
        low = lax.broadcasted_iota(jnp.int32, (16, LANES), 1) < HALF
        low_max = jnp.max(jnp.where(low, largest, 0.0), axis=1, keepdims=True)
        high_max = jnp.max(jnp.where(low, 0.0, largest), axis=1, keepdims=True)
        D[core, zl, 0] = delta
        D[core, zl, 1] = jnp.where(low, low_max, high_max) + 1e-6
        for k in range(1, 4):
            block = D.at[core, zl]
            remote(block, block, SD, SD, ((zl + k) % ZL) * 2 + core, fsdp).start()
        wait_bytes(R3.at[pl.ds(0, 11)], recv.at[Z0])

    @pl.when(zl >= OWN)
    def _():
        wait_bytes(R3.at[pl.ds(0, 12)], recv.at[Z0])

    for h in range(2):
        mine, other = along[h]
        for d in (2, 1, 3):
            dest = (other + d) % 4
            block = G.at[core, h, mine, other]
            remote(block, block, A1 + h, A1 + h, rep, second_peer(h, dest)).start()
    for h in range(2):
        mine, other = along[h]
        wait_bytes(G.at[core, h, mine, pl.ds(0, 3)], recv.at[A1 + h])
        for w, near, on, _ in ways(h):
            block = G.at[core, h, mine, on]
            remote(block, block, A2A + h, A2A + 2 * h + w, rep, first_peer(h, near)).start()
        for w, near, _, rest in ways(h):
            block = G.at[core, h, mine, rest]
            remote(block, block, A2A + h, A2B + 2 * h + w, rep, first_peer(h, near)).start()
        block = G.at[core, h, mine]
        remote(block, block, SC + h, SC + h, sibling, fsdp).start()

    @pl.when(zl < OWN)
    def _():
        wait_bytes(D.at[core, pl.ds(0, 2)], recv.at[SD])

    @pl.when(zl >= OWN)
    def _():
        wait_bytes(D.at[core], recv.at[SD])

    remote(D.at[core], D.at[core], SDS, SDS, sibling, fsdp).start()

    for h in range(2):
        back = ways(h)[1][1], ways(h)[0][1]
        for w, near, on, _ in ways(h):
            block = G.at[core, h, back[w], on]
            wait_bytes(block, recv.at[A2A + 2 * h + w])
            remote(block, block, A2A + h, A2R + 2 * h + w, rep, first_peer(h, near)).start()
            remote(block, block, SC + h, SC + h, sibling, fsdp).start()

    wait_bytes(D.at[1 - core], recv.at[SDS])
    state = ([], [], [])
    for c in range(2):
        for k in range(OWN):
            moment = 0.9 * MO[c, k] + D[c, k, 0]
            state[0].append(moment)
            state[1].append(M[c, k] - 0.7 * (D[c, k, 0] + 0.9 * moment))
            state[2].append(D[c, k, 1])
    moments, masters, scales = ([s[0:3], s[3:6]] for s in state)
    for tiles, d_out, g_out in ((moments, dmo_out, gmo_out), (masters, dm_out, gm_out)):
        for c in range(2):
            for k in range(2):
                row = 32 * c + 16 * k
                d_out[row : row + 16, :] = tiles[c][k]
        for g in range(2):
            for t in range(4):
                row = 8 * (t % 2) + 4 * g
                width = 128 if t < 3 else 64
                g_out[g, :, 128 * t : 128 * t + width] = tiles[t // 2][2][row : row + 4, :width]
    rows = jnp.concatenate([scales[c][k] for c in range(2) for k in range(2)], axis=0)
    lane64 = lax.broadcasted_iota(jnp.int32, (64, LANES), 1)
    pair = jnp.where(lane64 == 0, rows, pltpu.roll(rows, HALF, 1))
    ds_out[...] = pair.T[0:2, :]
    acc = jnp.zeros((8, LANES), F32)
    for t in range(4):
        tile = scales[t // 2][2][8 * (t % 2) : 8 * (t % 2) + 8]
        acc = jnp.where(lane8 == 2 * t, tile, acc)
        acc = jnp.where(lane8 == 2 * t + 1, pltpu.roll(tile, HALF, 1), acc)
    for g in range(2):
        gs_out[g, :, :] = acc[4 * g : 4 * g + 4, 0:7]

    for h in range(2):
        back = ways(h)[1][1], ways(h)[0][1]
        for w, _, _, rest in ways(h):
            block = G.at[core, h, back[w], rest]
            wait_bytes(block, recv.at[A2B + 2 * h + w])
            remote(block, block, SC + h, SC + h, sibling, fsdp).start()
    for h in range(2):
        far = (along[h][0] + 2) % 4
        for w, _, on, _ in ways(h):
            block = G.at[core, h, far, on]
            wait_bytes(block, recv.at[A2R + 2 * h + w])
            remote(block, block, SC + h, SC + h, sibling, fsdp).start()
    for h in range(2):
        wait_bytes(G.at[1 - core, h], recv.at[SC + h])
        for z2 in range(2):
            zh_ = 2 * h + z2
            for x_ in range(NX):
                gu_tiles = []
                for y_ in range(NY):
                    e1, e2 = (x_, y_) if h == 0 else (y_, x_)
                    col = ((zh_ * NX + x_) * NY + y_) * LANES
                    wide = []
                    for c in range(2):
                        for k in range(2):
                            row = 32 * c + 16 * k
                            dn_out[row : row + 16, col : col + LANES] = G[c, h, e1, e2, z2, k]
                        tile = G[c, h, e1, e2, z2, 2].astype(F32)
                        wide += [tile[0:8], tile[8:16]]
                    gu_tiles.append(wide)
                for yp in range(NY // 2):
                    even, odd = gu_tiles[2 * yp], gu_tiles[2 * yp + 1]
                    odd = pltpu.roll(jnp.concatenate(odd, axis=1), HALF, 1)
                    joined = jnp.where(lane8 < HALF, even[3], odd[:, 0:128])
                    full = jnp.concatenate(even[:3] + [joined, odd[:, 128:512]], axis=1)
                    col = ((zh_ * NX + x_) * NY + 2 * yp) * GUCOLS
                    for g in range(2):
                        gu_out[g, :, col : col + 2 * GUCOLS] = full[4 * g : 4 * g + 4].astype(BF)

    for h in range(2):
        wait_bytes(S.at[h, pl.ds(0, 3)], send.at[P1B + h])
        wait_bytes(R2.at[h, pl.ds(0, 7)], send.at[P2 + h])
        wait_bytes(G.at[core, h, 0, pl.ds(0, 3)], send.at[A1 + h])
        wait_bytes(G.at[core, h, pl.ds(0, 3)], send.at[A2A + h])
        wait_bytes(G.at[core, h], send.at[SC + h])
    wait_bytes(D.at[core], send.at[SDS])

    @pl.when(zl < OWN)
    def _():
        wait_bytes(R3.at[pl.ds(0, 22)], send.at[Z3])
        wait_bytes(R3.at[pl.ds(0, 15)], send.at[Z0])
        wait_bytes(D.at[core], send.at[SD])

    @pl.when(zl >= OWN)
    def _():
        wait_bytes(R3.at[pl.ds(0, 24)], send.at[Z3])


def place(*refs):
    n = (len(refs) - 1) // 2
    copies = [pltpu.make_async_copy(refs[i], refs[n + i], refs[-1].at[i]) for i in range(n)]
    for copy in copies:
        copy.start()
    for copy in copies:
        copy.wait()


def per_device(gu_pseudo, gu_master, gu_moment, down_pseudo, down_master, down_moment):
    shapes = (
        jax.ShapeDtypeStruct(gu_pseudo.shape[2:], BF),
        jax.ShapeDtypeStruct(down_pseudo.shape[2:], BF),
        jax.ShapeDtypeStruct(gu_master.shape, F32),
        jax.ShapeDtypeStruct(down_master.shape, F32),
        jax.ShapeDtypeStruct(gu_master.shape, F32),
        jax.ShapeDtypeStruct(down_master.shape, F32),
        jax.ShapeDtypeStruct(gu_master.shape[:2] + (7,), F32),
        jax.ShapeDtypeStruct((2, down_master.shape[0]), F32),
    )
    operands = [
        pltpu.with_memory_space_constraint(a, pltpu.HBM)
        for a in (gu_pseudo, gu_master, gu_moment, down_pseudo, down_master, down_moment)
    ]
    vmem = pl.BlockSpec(memory_space=pltpu.VMEM)
    hbm = pl.BlockSpec(memory_space=pl.ANY)
    results = pl.pallas_call(
        kernel,
        out_shape=shapes,
        in_specs=[hbm] * 6,
        out_specs=[vmem] * 8,
        scratch_shapes=[
            pltpu.VMEM(gu_pseudo.shape, BF),
            pltpu.VMEM(down_pseudo.shape, BF),
            pltpu.VMEM(gu_master.shape, F32),
            pltpu.VMEM(gu_master.shape, F32),
            pltpu.VMEM(down_master.shape, F32),
            pltpu.VMEM(down_master.shape, F32),
            pltpu.VMEM((2, 4, 4, 2, 2, 48, LANES), BF),
            pltpu.VMEM((2, 2, 2, 2, 2, 48, LANES), BF),
            pltpu.VMEM((2, 2, 4, 2, 2, 48, LANES), BF),
            pltpu.VMEM((2, 4, 2, 2, 48, LANES), BF),
            pltpu.VMEM((2, 8, 2, 48, LANES), BF),
            pltpu.VMEM((4, OWN, 2, 16, LANES), BF),
            pltpu.VMEM((32, 16, LANES), BF),
            pltpu.VMEM((2, OWN, 2, 16, LANES), F32),
            pltpu.VMEM((2, 2, 4, 4, 2, OWN, 16, LANES), BF),
            pltpu.VMEM((2, OWN, 16, LANES), F32),
            pltpu.VMEM((2, OWN, 16, LANES), F32),
            pltpu.SemaphoreType.DMA((NSEM,)),
            pltpu.SemaphoreType.DMA((NSEM,)),
            pltpu.SemaphoreType.DMA((6,)),
        ],
        compiler_params=pltpu.CompilerParams(
            collective_id=0, has_side_effects=True, vmem_limit_bytes=40 * MIB
        ),
    )(*operands)
    results = pl.pallas_call(
        place,
        out_shape=shapes,
        in_specs=[vmem] * 8,
        out_specs=[hbm] * 8,
        scratch_shapes=[pltpu.SemaphoreType.DMA((8,))],
        compiler_params=pltpu.CompilerParams(vmem_limit_bytes=40 * MIB),
    )(*results)
    return tuple(results[:7]) + (results[7].T,)


def solution(mesh):
    in_specs = (
        P("rep", "fsdp", None, None, None),
        P(None, None, "fsdp"),
        P(None, None, "fsdp"),
        P("rep", "fsdp", None, None),
        P(None, "fsdp"),
        P(None, "fsdp"),
    )
    out_specs = (
        P(),
        P(),
        P(None, None, "fsdp"),
        P(None, "fsdp"),
        P(None, None, "fsdp"),
        P(None, "fsdp"),
        P(None, None, "fsdp"),
        P(None, "fsdp"),
    )
    return jax.shard_map(
        per_device, mesh=mesh, in_specs=in_specs, out_specs=out_specs, check_vma=False
    )
```

time: 76.4 us -> 63.8 us (0.84)
  local copies, waits for them, and re-layouts: 10.6 us -> 0 us
  Pallas kernels: 64.7 us -> 63 us
    unnamed x19 -> x0, local copies, waits for them, and re-layouts: 9.95 us -> none
    pallas_call x1 -> x2, Pallas kernels: 64.7 us -> 63 us  [the longest x1 61.8 us: per_device(): pl.pallas_call(kernel, out_shape=shapes, in_specs=[hbm] * 6, out_specs=[v...]
where the time goes in v2:
time: 63.8 us; the launch traced here: 63.7 us
  Pallas kernels  63 us (99%)
  between operations  0.64 us (1%)
    pallas_call x1, Pallas kernels, per_device(): pl.pallas_call(kernel, out_shape=shapes, in_specs=[hbm] * 6, out_specs=[v...  61.8 us

profile of v2, /device:TPU:1, one launch (start us, length us, event | category | flops | bytes accessed | tf_op | source)
XLA Modules:
  0.0 63.7 jit_solution(11401508882368670761)
XLA Ops:
  0.6 61.8 %shard_map.125 = (bf16[2,4,28672]{2,1,0:T(4,128)(2,1)S(1)}, bf16[64,8192]{1,0:T(8,128)(2,1)S(1)}, f32[2,4,448]{2,1,0:T(4,128)S(1)}, f32[64,128]{1,0:T(8,128)S(1)...) custom-call(bf16[1,1,2,4,28672]{4,3,2,1,0:T(4,128)(2,1)} %gu_ref.1, ...), custom_call_target="tpu_custom_call" | custom-call | tf_op jit(solution)/shard_map/pallas_call | solution.py:379
  62.5 1.2 %shard_map.126 = (bf16[2,4,28672]{2,1,0:T(4,128)(2,1)}, bf16[64,8192]{1,0:T(8,128)(2,1)}, f32[2,4,448]{2,1,0:T(4,128)}, f32[64,128]{1,0:T(8,128)}, f32[2,4,448]{...) custom-call(bf16[2,4,28672]{2,1,0:T(4,128)(2,1)S(1)} %get-tuple-element.24.refs_0_, ...), custom_call_target="tpu_custom_call" | custom-call | tf_op jit(solution)/shard_map/pallas_call | solution.py:410

commit v3 on v2

v3 whole, which is shorter than its diff:
```python
import jax
import jax.numpy as jnp
from jax import lax
from jax.experimental import pallas as pl
from jax.experimental.pallas import tpu as pltpu
from jax.sharding import PartitionSpec as P

NX = 4
NY = 4
ZH = 4
ZL = 4
LANES = 128
HALF = 64
GUCOLS = 448
OWN = 3
BF = jnp.bfloat16
F32 = jnp.float32
MIB = 1024 * 1024

P1A, P1B, P2, Z3, Z0, SD, SDS, A1, A2, SC = 0, 8, 12, 16, 17, 19, 20, 21, 25, 37
NSEM = 41


def kernel(
    gu_ref, gm_ref, gmo_ref, dn_ref, dm_ref, dmo_ref,
    gu_out, dn_out, gm_out, dm_out, gmo_out, dmo_out, gs_out, ds_out,
    gu_in, dn_in, gm_in, gmo_in, dm_in, dmo_in,
    S, RA, R1, PS, R2, Q, R3, D, G, M, MO, send, recv, local, line,
):
    rep = lax.axis_index("rep")
    fsdp = lax.axis_index("fsdp")
    zl, core = rep // 2, rep % 2
    zh, x, y = fsdp // (NX * NY), (fsdp // NY) % NX, fsdp % NY
    z = zh * ZL + zl
    along = ((x, y), (y, x))
    sibling = zl * 2 + (1 - core)
    pairs = [(g, h) for g in range(2) for h in range(2)]

    def fs(zh_, x_, y_):
        return (zh_ * NX + x_) * NY + y_

    def first_peer(h, d):
        return fs(zh, d, y) if h == 0 else fs(zh, x, d)

    def second_peer(h, d):
        return fs(zh, x, d) if h == 0 else fs(zh, d, y)

    def on_line(oz):
        return (oz % ZL) * 2 + core, fs(oz // ZL, x, y)

    def remote(src, dst, out, sem, rep_, fsdp_):
        return pltpu.make_async_remote_copy(
            src_ref=src, dst_ref=dst, send_sem=send.at[out], recv_sem=recv.at[sem],
            device_id={"rep": rep_, "fsdp": fsdp_}, device_id_type=pl.DeviceIdType.MESH,
        )

    def wait_bytes(ref, sem):
        pltpu.make_async_copy(ref, ref, sem).wait()

    loads = [
        pltpu.make_async_copy(src, dst, local.at[i])
        for i, (src, dst) in enumerate(
            (
                (dn_ref, dn_in), (gu_ref, gu_in), (dm_ref, dm_in), (dmo_ref, dmo_in),
                (gm_ref, gm_in), (gmo_ref, gmo_in),
            )
        )
    ]
    for load in loads:
        load.start()

    def signal(sem, rep_, fsdp_):
        pl.semaphore_signal(
            sem, inc=1, device_id={"rep": rep_, "fsdp": fsdp_}, device_id_type=pl.DeviceIdType.MESH
        )

    barrier = pltpu.get_barrier_semaphore()
    for r in (rep, sibling):
        for d in (2, 1, 3):
            signal(barrier, r, fs(zh, (x + d) % 4, y))
            signal(barrier, r, fs(zh, x, (y + d) % 4))
    for d in (1, 15):
        signal(barrier, *on_line((z + d) % 16))
    signal(barrier, sibling, fsdp)

    lane = lax.broadcasted_iota(jnp.int32, (8, 512), 1)
    lane8 = lax.broadcasted_iota(jnp.int32, (8, LANES), 1)

    def arrange(g):
        for h in range(2):
            zh_ = 2 * h + g
            for x_ in range(NX):
                for y_ in range(NY):
                    d1, d2 = (x_, y_) if h == 0 else (y_, x_)
                    col = ((zh_ * NX + x_) * NY + y_) * LANES
                    for c in range(2):
                        S[g, h, d1, d2, c, 0:32, :] = dn_in[0, 0, 32 * c : 32 * c + 32, col : col + LANES]
                for yp in range(NY // 2):
                    col = ((zh_ * NX + x_) * NY + 2 * yp) * GUCOLS
                    both = jnp.concatenate(
                        [gu_in[0, 0, i, :, col : col + 2 * GUCOLS].astype(F32) for i in range(2)], axis=0
                    )
                    odd = pltpu.roll(both[:, 384:896], 512 - HALF, 1)
                    for o, part in enumerate((both[:, 0:512], odd)):
                        part = jnp.where(lane < GUCOLS, part, 0.0)
                        y_ = 2 * yp + o
                        d1, d2 = (x_, y_) if h == 0 else (y_, x_)
                        for c in range(2):
                            two = jnp.concatenate(
                                [part[:, 256 * c : 256 * c + 128], part[:, 256 * c + 128 : 256 * c + 256]], axis=0
                            )
                            S[g, h, d1, d2, c, 32:48, :] = two.astype(BF)

    def ways(h):
        mine = along[h][0]
        return (
            (0, (mine + 1) % 4, pl.ds(0, 2), pl.ds(2, 2)),
            (1, (mine + 3) % 4, pl.ds(2, 2), pl.ds(0, 2)),
        )

    def first_axis(g):
        for h in range(2):
            far = (along[h][0] + 2) % 4
            for w, near, on, _ in ways(h):
                remote(
                    S.at[g, h, far, on], RA.at[g, h, w], P1B + 2 * g + h, P1A + 4 * g + 2 * h + w,
                    rep, first_peer(h, near),
                ).start()
        for h in range(2):
            for w, near, _, rest in ways(h):
                sem = P1B + 2 * g + h
                remote(S.at[g, h, near, rest], R1.at[g, h, w, rest], sem, sem, rep, first_peer(h, near)).start()

    def pass_on(g):
        for h in range(2):
            for w, near, on, _ in ways(h):
                wait_bytes(RA.at[g, h, w], recv.at[P1A + 4 * g + 2 * h + w])
                S[g, h, near, on] = (S[g, h, near, on].astype(F32) + RA[g, h, w].astype(F32)).astype(BF)
                sem = P1B + 2 * g + h
                remote(S.at[g, h, near, on], R1.at[g, h, w, on], sem, sem, rep, first_peer(h, near)).start()

    def second_axis(g):
        for h in range(2):
            mine, other = along[h]
            sem = P2 + 2 * g + h
            wait_bytes(R1.at[g, h], recv.at[P1B + 2 * g + h])
            for d in (2, 1, 3, 0):
                dest = (other + d) % 4
                acc = S[g, h, mine, dest].astype(F32) + R1[g, h, 0, dest].astype(F32)
                acc = acc + R1[g, h, 1, dest].astype(F32)
                PS[g, h, dest] = acc.astype(BF)
                if d:
                    to = second_peer(h, dest)
                    slot = R2.at[g, h, 2 * (d - 1) + core]
                    remote(PS.at[g, h, dest, core], slot, sem, sem, rep, to).start()
                    remote(PS.at[g, h, dest, 1 - core], slot, sem, sem, sibling, to).start()
                else:
                    remote(PS.at[g, h, dest, 1 - core], R2.at[g, h, 6 + core], sem, sem, sibling, fsdp).start()
                    R2[g, h, 6 + core] = PS[g, h, dest, core]

    def to_owners(g):
        for h in range(2):
            to = 2 * h + g
            wait_bytes(R2.at[g, h, pl.ds(0, 7)], recv.at[P2 + 2 * g + h])
            for c in range(2):
                acc = R2[g, h, c].astype(F32)
                for i in range(1, 4):
                    acc = acc + R2[g, h, 2 * i + c].astype(F32)
                acc = acc.astype(BF).reshape(OWN, 16, LANES)
                for k in range(OWN):
                    Q[to, k, c] = acc[k]
            for k in range(OWN):
                copy = remote(Q.at[to, k], R3.at[pl.ds(2 * z, 2)], Z3, Z3, 2 * k + core, fs(to, x, y))
                pl.when(jnp.logical_or(zh != to, zl != k))(copy.start)

    loads[0].wait()
    loads[1].wait()
    arrange(0)
    pl.semaphore_wait(barrier, 15)
    first_axis(0)
    arrange(1)
    first_axis(1)

    for i, d in enumerate((1, 2, 4)):
        signal(line.at[i], *on_line((z + d) % 16))
        signal(line.at[i], *on_line((z + 16 - d) % 16))
        pl.semaphore_wait(line.at[i], 2)
        if i == 0:
            for load in loads[2:]:
                load.wait()
            for g_ref, d_ref, out in ((gm_in, dm_in, M), (gmo_in, dmo_in, MO)):
                for c in range(2):
                    for k in range(2):
                        row = 32 * c + 16 * k
                        out[c, k] = d_ref[row : row + 16, :]
                for j in range(2):
                    for t in range(4):
                        row = 8 * (t % 2) + 4 * j
                        if t < 3:
                            out[t // 2, 2, row : row + 4, :] = g_ref[j, :, 128 * t : 128 * t + 128]
                        else:
                            out[1, 2, row : row + 4, :] = jnp.concatenate(
                                [g_ref[j, :, 384:448], jnp.zeros((4, HALF), F32)], axis=1
                            )
        if i == 1:
            pass_on(0)
    pass_on(1)
    second_axis(0)
    second_axis(1)
    to_owners(0)
    to_owners(1)

    hh, gg = zh // 2, zh % 2
    d1 = jnp.where(hh == 0, x, y)
    d2 = jnp.where(hh == 0, y, x)

    @pl.when(zl < OWN)
    def _():
        R3[pl.ds(2 * z, 2)] = Q[zh, zl]
        wait_bytes(R3.at[pl.ds(0, 30)], recv.at[Z3])
        largest = jnp.zeros((16, LANES), F32)
        total = jnp.zeros((16, LANES), F32)
        for r in range(8):
            part = R3[r].astype(F32)
            for k in range(1, 4):
                part = part + R3[8 * k + r].astype(F32)
            largest = jnp.maximum(largest, jnp.abs(part))
            total = total + part
        delta = total / 8
        moment = 0.9 * MO[core, zl] + delta
        master = M[core, zl] - 0.7 * (delta + 0.9 * moment)
        mine = G.at[core, gg, hh, d1, d2, zl]
        mine[...] = master.astype(BF)

        def spread(k, carry):
            oz = (z + 8 + jnp.where(k % 2 == 0, k // 2, 16 - (k + 1) // 2)) % 16
            remote(mine, mine, Z0, Z0 + gg, *on_line(oz)).start()
            return carry

        lax.fori_loop(0, 15, spread, 0)
        low = lax.broadcasted_iota(jnp.int32, (16, LANES), 1) < HALF
        low_max = jnp.max(jnp.where(low, largest, 0.0), axis=1, keepdims=True)
        high_max = jnp.max(jnp.where(low, 0.0, largest), axis=1, keepdims=True)
        D[core, zl, 0] = delta
        D[core, zl, 1] = jnp.where(low, low_max, high_max) + 1e-6
        for k in range(1, 4):
            block = D.at[core, zl]
            remote(block, block, SD, SD, ((zl + k) % ZL) * 2 + core, fsdp).start()

    def gather_second(g):
        owner = jnp.logical_and(zl < OWN, gg == g)

        @pl.when(owner)
        def _():
            wait_bytes(R3.at[pl.ds(0, 5)], recv.at[Z0 + g])

        @pl.when(jnp.logical_not(owner))
        def _():
            wait_bytes(R3.at[pl.ds(0, 6)], recv.at[Z0 + g])

        for h in range(2):
            mine, other = along[h]
            sem = A1 + 2 * g + h
            for d in (2, 1, 3):
                block = G.at[core, g, h, mine, other]
                remote(block, block, sem, sem, rep, second_peer(h, (other + d) % 4)).start()

    def to_sibling(g, h, d):
        block = G.at[core, g, h, d]
        remote(block, block, SC + 2 * g + h, SC + 2 * g + h, sibling, fsdp).start()

    def gather_first(g):
        for h in range(2):
            mine, other = along[h]
            wait_bytes(G.at[core, g, h, mine, pl.ds(0, 3)], recv.at[A1 + 2 * g + h])
            for d in (2, 1, 3):
                block = G.at[core, g, h, mine]
                remote(
                    block, block, A2 + 6 * g + 3 * h, A2 + 6 * g + 3 * h + d - 1,
                    rep, first_peer(h, (mine + d) % 4),
                ).start()
            to_sibling(g, h, mine)

    def share(g):
        for d in (1, 3, 2):
            for h in range(2):
                source = (along[h][0] + 4 - d) % 4
                wait_bytes(G.at[core, g, h, source], recv.at[A2 + 6 * g + 3 * h + d - 1])
                to_sibling(g, h, source)

    gather_second(0)
    gather_second(1)
    gather_first(0)

    @pl.when(zl < OWN)
    def _():
        wait_bytes(D.at[core, pl.ds(0, 2)], recv.at[SD])

    @pl.when(zl >= OWN)
    def _():
        wait_bytes(D.at[core], recv.at[SD])

    remote(D.at[core], D.at[core], SDS, SDS, sibling, fsdp).start()

    gather_first(1)
    share(0)

    wait_bytes(D.at[1 - core], recv.at[SDS])
    state = ([], [], [])
    for c in range(2):
        for k in range(OWN):
            moment = 0.9 * MO[c, k] + D[c, k, 0]
            state[0].append(moment)
            state[1].append(M[c, k] - 0.7 * (D[c, k, 0] + 0.9 * moment))
            state[2].append(D[c, k, 1])
    moments, masters, scales = ([s[0:3], s[3:6]] for s in state)
    for tiles, d_out, g_out in ((moments, dmo_out, gmo_out), (masters, dm_out, gm_out)):
        for c in range(2):
            for k in range(2):
                row = 32 * c + 16 * k
                d_out[row : row + 16, :] = tiles[c][k]
        for j in range(2):
            for t in range(4):
                row = 8 * (t % 2) + 4 * j
                width = 128 if t < 3 else 64
                g_out[j, :, 128 * t : 128 * t + width] = tiles[t // 2][2][row : row + 4, :width]
    rows = jnp.concatenate([scales[c][k] for c in range(2) for k in range(2)], axis=0)
    lane64 = lax.broadcasted_iota(jnp.int32, (64, LANES), 1)
    pair = jnp.where(lane64 == 0, rows, pltpu.roll(rows, HALF, 1))
    ds_out[...] = pair.T[0:2, :]
    acc = jnp.zeros((8, LANES), F32)
    for t in range(4):
        tile = scales[t // 2][2][8 * (t % 2) : 8 * (t % 2) + 8]
        acc = jnp.where(lane8 == 2 * t, tile, acc)
        acc = jnp.where(lane8 == 2 * t + 1, pltpu.roll(tile, HALF, 1), acc)
    for j in range(2):
        gs_out[j, :, :] = acc[4 * j : 4 * j + 4, 0:7]

    def write(g, h):
        zh_ = 2 * h + g
        wait_bytes(G.at[1 - core, g, h], recv.at[SC + 2 * g + h])
        for x_ in range(NX):
            gu_tiles = []
            for y_ in range(NY):
                e1, e2 = (x_, y_) if h == 0 else (y_, x_)
                col = ((zh_ * NX + x_) * NY + y_) * LANES
                wide = []
                for c in range(2):
                    for k in range(2):
                        row = 32 * c + 16 * k
                        dn_out[row : row + 16, col : col + LANES] = G[c, g, h, e1, e2, k]
                    tile = G[c, g, h, e1, e2, 2].astype(F32)
                    wide += [tile[0:8], tile[8:16]]
                gu_tiles.append(wide)
            for yp in range(NY // 2):
                even, odd = gu_tiles[2 * yp], gu_tiles[2 * yp + 1]
                odd = pltpu.roll(jnp.concatenate(odd, axis=1), HALF, 1)
                joined = jnp.where(lane8 < HALF, even[3], odd[:, 0:128])
                full = jnp.concatenate(even[:3] + [joined, odd[:, 128:512]], axis=1)
                col = ((zh_ * NX + x_) * NY + 2 * yp) * GUCOLS
                for j in range(2):
                    gu_out[j, :, col : col + 2 * GUCOLS] = full[4 * j : 4 * j + 4].astype(BF)

    write(0, 0)
    write(0, 1)
    share(1)
    write(1, 0)
    write(1, 1)

    for g, h in pairs:
        i = 2 * g + h
        wait_bytes(S.at[g, h, pl.ds(0, 3)], send.at[P1B + i])
        wait_bytes(R2.at[g, h, pl.ds(0, 7)], send.at[P2 + i])
        wait_bytes(G.at[core, g, h, 0, pl.ds(0, 3)], send.at[A1 + i])
        wait_bytes(G.at[core, g, h, pl.ds(0, 3)], send.at[A2 + 3 * i])
        wait_bytes(G.at[core, g, h], send.at[SC + i])
    wait_bytes(D.at[core], send.at[SDS])

    @pl.when(zl < OWN)
    def _():
        wait_bytes(R3.at[pl.ds(0, 22)], send.at[Z3])
        wait_bytes(R3.at[pl.ds(0, 15)], send.at[Z0])
        wait_bytes(D.at[core], send.at[SD])

    @pl.when(zl >= OWN)
    def _():
        wait_bytes(R3.at[pl.ds(0, 24)], send.at[Z3])


def place(*refs):
    n = (len(refs) - 1) // 2
    copies = [pltpu.make_async_copy(refs[i], refs[n + i], refs[-1].at[i]) for i in range(n)]
    for copy in copies:
        copy.start()
    for copy in copies:
        copy.wait()


def per_device(gu_pseudo, gu_master, gu_moment, down_pseudo, down_master, down_moment):
    shapes = (
        jax.ShapeDtypeStruct(gu_pseudo.shape[2:], BF),
        jax.ShapeDtypeStruct(down_pseudo.shape[2:], BF),
        jax.ShapeDtypeStruct(gu_master.shape, F32),
        jax.ShapeDtypeStruct(down_master.shape, F32),
        jax.ShapeDtypeStruct(gu_master.shape, F32),
        jax.ShapeDtypeStruct(down_master.shape, F32),
        jax.ShapeDtypeStruct(gu_master.shape[:2] + (7,), F32),
        jax.ShapeDtypeStruct((2, down_master.shape[0]), F32),
    )
    operands = [
        pltpu.with_memory_space_constraint(a, pltpu.HBM)
        for a in (gu_pseudo, gu_master, gu_moment, down_pseudo, down_master, down_moment)
    ]
    vmem = pl.BlockSpec(memory_space=pltpu.VMEM)
    hbm = pl.BlockSpec(memory_space=pl.ANY)
    results = pl.pallas_call(
        kernel,
        out_shape=shapes,
        in_specs=[hbm] * 6,
        out_specs=[vmem] * 8,
        scratch_shapes=[
            pltpu.VMEM(gu_pseudo.shape, BF),
            pltpu.VMEM(down_pseudo.shape, BF),
            pltpu.VMEM(gu_master.shape, F32),
            pltpu.VMEM(gu_master.shape, F32),
            pltpu.VMEM(down_master.shape, F32),
            pltpu.VMEM(down_master.shape, F32),
            pltpu.VMEM((2, 2, 4, 4, 2, 48, LANES), BF),
            pltpu.VMEM((2, 2, 2, 2, 2, 48, LANES), BF),
            pltpu.VMEM((2, 2, 2, 4, 2, 48, LANES), BF),
            pltpu.VMEM((2, 2, 4, 2, 48, LANES), BF),
            pltpu.VMEM((2, 2, 8, 48, LANES), BF),
            pltpu.VMEM((4, OWN, 2, 16, LANES), BF),
            pltpu.VMEM((32, 16, LANES), BF),
            pltpu.VMEM((2, OWN, 2, 16, LANES), F32),
            pltpu.VMEM((2, 2, 2, 4, 4, OWN, 16, LANES), BF),
            pltpu.VMEM((2, OWN, 16, LANES), F32),
            pltpu.VMEM((2, OWN, 16, LANES), F32),
            pltpu.SemaphoreType.DMA((NSEM,)),
            pltpu.SemaphoreType.DMA((NSEM,)),
            pltpu.SemaphoreType.DMA((6,)),
            pltpu.SemaphoreType.REGULAR((3,)),
        ],
        compiler_params=pltpu.CompilerParams(
            collective_id=0, has_side_effects=True, vmem_limit_bytes=40 * MIB
        ),
    )(*operands)
    results = pl.pallas_call(
        place,
        out_shape=shapes,
        in_specs=[vmem] * 8,
        out_specs=[hbm] * 8,
        scratch_shapes=[pltpu.SemaphoreType.DMA((8,))],
        compiler_params=pltpu.CompilerParams(vmem_limit_bytes=40 * MIB),
    )(*results)
    return tuple(results[:7]) + (results[7].T,)


def solution(mesh):
    in_specs = (
        P("rep", "fsdp", None, None, None),
        P(None, None, "fsdp"),
        P(None, None, "fsdp"),
        P("rep", "fsdp", None, None),
        P(None, "fsdp"),
        P(None, "fsdp"),
    )
    out_specs = (
        P(),
        P(),
        P(None, None, "fsdp"),
        P(None, "fsdp"),
        P(None, None, "fsdp"),
        P(None, "fsdp"),
        P(None, None, "fsdp"),
        P(None, "fsdp"),
    )
    return jax.shard_map(
        per_device, mesh=mesh, in_specs=in_specs, out_specs=out_specs, check_vma=False
    )
```

time: 63.8 us -> 55.5 us (0.87)
  Pallas kernels: 63 us -> 54.7 us
    pallas_call x1, Pallas kernels: 61.8 us -> 53.5 us  [per_device(): pl.pallas_call(kernel, out_shape=shapes, in_specs=[hbm] * 6, out_specs=[v...]
where the time goes in v3:
time: 55.5 us; the launch traced here: 55.4 us
  Pallas kernels  54.7 us (99%)
  between operations  0.64 us (1%)
    pallas_call x1, Pallas kernels, per_device(): pl.pallas_call(kernel, out_shape=shapes, in_specs=[hbm] * 6, out_specs=[v...  53.5 us
    pallas_call x1, Pallas kernels, per_device(): pl.pallas_call(place, out_shape=shapes, in_specs=[vmem] * 8, out_specs=[h...  1.21 us

profile of v3, /device:TPU:1, one launch (start us, length us, event | category | flops | bytes accessed | tf_op | source)
XLA Modules:
  0.0 55.4 jit_solution(10471168886977969203)
XLA Ops:
  0.6 53.5 %shard_map.125 = (bf16[2,4,28672]{2,1,0:T(4,128)(2,1)S(1)}, bf16[64,8192]{1,0:T(8,128)(2,1)S(1)}, f32[2,4,448]{2,1,0:T(4,128)S(1)}, f32[64,128]{1,0:T(8,128)S(1)...) custom-call(bf16[1,1,2,4,28672]{4,3,2,1,0:T(4,128)(2,1)} %gu_ref.1, ...), custom_call_target="tpu_custom_call" | custom-call | tf_op jit(solution)/shard_map/pallas_call | solution.py:416
  54.2 1.2 %shard_map.126 = (bf16[2,4,28672]{2,1,0:T(4,128)(2,1)}, bf16[64,8192]{1,0:T(8,128)(2,1)}, f32[2,4,448]{2,1,0:T(4,128)}, f32[64,128]{1,0:T(8,128)}, f32[2,4,448]{...) custom-call(bf16[2,4,28672]{2,1,0:T(4,128)(2,1)S(1)} %get-tuple-element.24.refs_0_, ...), custom_call_target="tpu_custom_call" | custom-call | tf_op jit(solution)/shard_map/pallas_call | solution.py:448

commit v4 on v3

--- a/solution.py
+++ b/solution.py
@@ -13,6 +13,8 @@
 HALF = 64
 GUCOLS = 448
 OWN = 3
+SHARD = ((0, 2), (1, 3))
+OWNER = (0, 2)
 BF = jnp.bfloat16
 F32 = jnp.float32
 MIB = 1024 * 1024
@@ -34,6 +36,7 @@
     z = zh * ZL + zl
     along = ((x, y), (y, x))
     sibling = zl * 2 + (1 - core)
+    owner = zl == OWNER[0] + core * (OWNER[1] - OWNER[0])
     pairs = [(g, h) for g in range(2) for h in range(2)]
 
     def fs(zh_, x_, y_):
@@ -74,21 +77,34 @@
             sem, inc=1, device_id={"rep": rep_, "fsdp": fsdp_}, device_id_type=pl.DeviceIdType.MESH
         )
 
+    near = [
+        (rep, fs(zh, (x + 1) % 4, y)), (rep, fs(zh, (x + 3) % 4, y)),
+        (rep, fs(zh, x, (y + 1) % 4)), (rep, fs(zh, x, (y + 3) % 4)),
+    ]
     barrier = pltpu.get_barrier_semaphore()
-    for r in (rep, sibling):
-        for d in (2, 1, 3):
-            signal(barrier, r, fs(zh, (x + d) % 4, y))
-            signal(barrier, r, fs(zh, x, (y + d) % 4))
-    for d in (1, 15):
-        signal(barrier, *on_line((z + d) % 16))
-    signal(barrier, sibling, fsdp)
+    for peer in near + [(sibling, fsdp), on_line((z + 1) % 16), on_line((z + 15) % 16)]:
+        signal(barrier, *peer)
+
+    rounds = (
+        near + [on_line((z + 1) % 16), on_line((z + 15) % 16)],
+        [on_line((z + 2) % 16), on_line((z + 14) % 16)],
+        [on_line((z + 4) % 16), on_line((z + 12) % 16)],
+        [(sibling, fsdp)],
+    )
+
+    def tell(i):
+        for peer in rounds[i]:
+            signal(line.at[i], *peer)
+
+    def hear(i):
+        pl.semaphore_wait(line.at[i], len(rounds[i]))
 
     lane = lax.broadcasted_iota(jnp.int32, (8, 512), 1)
     lane8 = lax.broadcasted_iota(jnp.int32, (8, LANES), 1)
 
     def arrange(g):
         for h in range(2):
-            zh_ = 2 * h + g
+            zh_ = SHARD[g][h]
             for x_ in range(NX):
                 for y_ in range(NY):
                     d1, d2 = (x_, y_) if h == 0 else (y_, x_)
@@ -118,7 +134,7 @@
             (1, (mine + 3) % 4, pl.ds(2, 2), pl.ds(0, 2)),
         )
 
-    def first_axis(g):
+    def ahead(g):
         for h in range(2):
             far = (along[h][0] + 2) % 4
             for w, near, on, _ in ways(h):
@@ -126,6 +142,8 @@
                     S.at[g, h, far, on], RA.at[g, h, w], P1B + 2 * g + h, P1A + 4 * g + 2 * h + w,
                     rep, first_peer(h, near),
                 ).start()
+
+    def rest_of(g):
         for h in range(2):
             for w, near, _, rest in ways(h):
                 sem = P1B + 2 * g + h
@@ -150,76 +168,69 @@
                 acc = acc + R1[g, h, 1, dest].astype(F32)
                 PS[g, h, dest] = acc.astype(BF)
                 if d:
-                    to = second_peer(h, dest)
-                    slot = R2.at[g, h, 2 * (d - 1) + core]
-                    remote(PS.at[g, h, dest, core], slot, sem, sem, rep, to).start()
-                    remote(PS.at[g, h, dest, 1 - core], slot, sem, sem, sibling, to).start()
-                else:
-                    remote(PS.at[g, h, dest, 1 - core], R2.at[g, h, 6 + core], sem, sem, sibling, fsdp).start()
-                    R2[g, h, 6 + core] = PS[g, h, dest, core]
+                    remote(PS.at[g, h, dest], R2.at[g, h, d - 1], sem, sem, rep, second_peer(h, dest)).start()
 
     def to_owners(g):
         for h in range(2):
-            to = 2 * h + g
-            wait_bytes(R2.at[g, h, pl.ds(0, 7)], recv.at[P2 + 2 * g + h])
+            to = SHARD[g][h]
+            wait_bytes(R2.at[g, h], recv.at[P2 + 2 * g + h])
+            acc = PS[g, h, along[h][1]].astype(F32)
+            for i in range(3):
+                acc = acc + R2[g, h, i].astype(F32)
+            Q[to] = acc.astype(BF)
             for c in range(2):
-                acc = R2[g, h, c].astype(F32)
-                for i in range(1, 4):
-                    acc = acc + R2[g, h, 2 * i + c].astype(F32)
-                acc = acc.astype(BF).reshape(OWN, 16, LANES)
-                for k in range(OWN):
-                    Q[to, k, c] = acc[k]
-            for k in range(OWN):
-                copy = remote(Q.at[to, k], R3.at[pl.ds(2 * z, 2)], Z3, Z3, 2 * k + core, fs(to, x, y))
-                pl.when(jnp.logical_or(zh != to, zl != k))(copy.start)
+                copy = remote(Q.at[to, c], R3.at[2 * z + core], Z3, Z3, 2 * OWNER[c] + c, fs(to, x, y))
+                pl.when(jnp.logical_or(fsdp != fs(to, x, y), rep != 2 * OWNER[c] + c))(copy.start)
 
     loads[0].wait()
     loads[1].wait()
     arrange(0)
-    pl.semaphore_wait(barrier, 15)
-    first_axis(0)
+    pl.semaphore_wait(barrier, 7)
+    ahead(0)
     arrange(1)
-    first_axis(1)
-
-    for i, d in enumerate((1, 2, 4)):
-        signal(line.at[i], *on_line((z + d) % 16))
-        signal(line.at[i], *on_line((z + 16 - d) % 16))
-        pl.semaphore_wait(line.at[i], 2)
-        if i == 0:
-            for load in loads[2:]:
-                load.wait()
-            for g_ref, d_ref, out in ((gm_in, dm_in, M), (gmo_in, dmo_in, MO)):
-                for c in range(2):
-                    for k in range(2):
-                        row = 32 * c + 16 * k
-                        out[c, k] = d_ref[row : row + 16, :]
-                for j in range(2):
-                    for t in range(4):
-                        row = 8 * (t % 2) + 4 * j
-                        if t < 3:
-                            out[t // 2, 2, row : row + 4, :] = g_ref[j, :, 128 * t : 128 * t + 128]
-                        else:
-                            out[1, 2, row : row + 4, :] = jnp.concatenate(
-                                [g_ref[j, :, 384:448], jnp.zeros((4, HALF), F32)], axis=1
-                            )
-        if i == 1:
-            pass_on(0)
+    ahead(1)
+    rest_of(0)
+    rest_of(1)
+    tell(0)
+    hear(0)
+    tell(1)
+    pass_on(0)
     pass_on(1)
+    for load in loads[2:]:
+        load.wait()
+    for g_ref, d_ref, out in ((gm_in, dm_in, M), (gmo_in, dmo_in, MO)):
+        for c in range(2):
+            for k in range(2):
+                row = 32 * c + 16 * k
+                out[c, 16 * k : 16 * k + 16, :] = d_ref[row : row + 16, :]
+        for j in range(2):
+            for t in range(4):
+                row = 8 * (t % 2) + 4 * j
+                if t < 3:
+                    out[t // 2, 32 + row : 36 + row, :] = g_ref[j, :, 128 * t : 128 * t + 128]
+                else:
+                    out[1, 32 + row : 36 + row, :] = jnp.concatenate(
+                        [g_ref[j, :, 384:448], jnp.zeros((4, HALF), F32)], axis=1
+                    )
+    hear(1)
+    tell(2)
     second_axis(0)
     second_axis(1)
+    hear(2)
+    tell(3)
+    hear(3)
     to_owners(0)
     to_owners(1)
 
     hh, gg = zh // 2, zh % 2
     d1 = jnp.where(hh == 0, x, y)
-    d2 = jnp.where(hh == 0, y, x)
-
-    @pl.when(zl < OWN)
+
+    @pl.when(owner)
     def _():
-        R3[pl.ds(2 * z, 2)] = Q[zh, zl]
-        wait_bytes(R3.at[pl.ds(0, 30)], recv.at[Z3])
-        largest = jnp.zeros((16, LANES), F32)
-        total = jnp.zeros((16, LANES), F32)
+        R3[2 * z + core] = Q[zh, core]
+        wait_bytes(R3.at[pl.ds(0, 31)], recv.at[Z3])
+        largest = jnp.zeros((48, LANES), F32)
+        total = jnp.zeros((48, LANES), F32)
         for r in range(8):
             part = R3[r].astype(F32)
             for k in range(1, 4):
@@ -227,43 +238,42 @@
             largest = jnp.maximum(largest, jnp.abs(part))
             total = total + part
         delta = total / 8
-        moment = 0.9 * MO[core, zl] + delta
-        master = M[core, zl] - 0.7 * (delta + 0.9 * moment)
-        mine = G.at[core, gg, hh, d1, d2, zl]
+        moment = 0.9 * MO[core] + delta
+        master = M[core] - 0.7 * (delta + 0.9 * moment)
+        mine = G.at[core, gg, hh, d1, 0]
         mine[...] = master.astype(BF)
-
-        def spread(k, carry):
-            oz = (z + 8 + jnp.where(k % 2 == 0, k // 2, 16 - (k + 1) // 2)) % 16
-            remote(mine, mine, Z0, Z0 + gg, *on_line(oz)).start()
-            return carry
-
-        lax.fori_loop(0, 15, spread, 0)
-        low = lax.broadcasted_iota(jnp.int32, (16, LANES), 1) < HALF
+        for k in (8, 7, 9, 6, 10, 5, 11, 4, 12, 3, 13, 2, 14, 1, 15):
+            remote(mine, mine, Z0, Z0 + gg, *on_line((z + k) % 16)).start()
+        low = lax.broadcasted_iota(jnp.int32, (48, LANES), 1) < HALF
         low_max = jnp.max(jnp.where(low, largest, 0.0), axis=1, keepdims=True)
         high_max = jnp.max(jnp.where(low, 0.0, largest), axis=1, keepdims=True)
-        D[core, zl, 0] = delta
-        D[core, zl, 1] = jnp.where(low, low_max, high_max) + 1e-6
-        for k in range(1, 4):
-            block = D.at[core, zl]
-            remote(block, block, SD, SD, ((zl + k) % ZL) * 2 + core, fsdp).start()
+        D[core, 0] = delta
+        D[core, 1] = jnp.where(low, low_max, high_max) + 1e-6
 
     def gather_second(g):
-        owner = jnp.logical_and(zl < OWN, gg == g)
-
-        @pl.when(owner)
+        made = jnp.logical_and(owner, gg == g)
+
+        @pl.when(made)
         def _():
-            wait_bytes(R3.at[pl.ds(0, 5)], recv.at[Z0 + g])
-
-        @pl.when(jnp.logical_not(owner))
+            wait_bytes(R3.at[0], recv.at[Z0 + g])
+
+        @pl.when(jnp.logical_not(made))
         def _():
-            wait_bytes(R3.at[pl.ds(0, 6)], recv.at[Z0 + g])
+            wait_bytes(R3.at[pl.ds(0, 2)], recv.at[Z0 + g])
 
         for h in range(2):
             mine, other = along[h]
             sem = A1 + 2 * g + h
+            block = G.at[core, g, h, mine, 0]
             for d in (2, 1, 3):
-                block = G.at[core, g, h, mine, other]
-                remote(block, block, sem, sem, rep, second_peer(h, (other + d) % 4)).start()
+                to = second_peer(h, (other + d) % 4)
+                remote(block, G.at[core, g, h, mine, 4 - d], sem, sem, rep, to).start()
+        for h in range(2):
+            mine = along[h][0]
+            block = G.at[core, g, h, mine, 0]
+            for d in (2, 1, 3):
+                to = first_peer(h, (mine + d) % 4)
+                remote(block, block, A1 + 2 * g + h, A2 + 6 * g + 3 * h + d - 1, rep, to).start()
 
     def to_sibling(g, h, d):
         block = G.at[core, g, h, d]
@@ -272,9 +282,9 @@
     def gather_first(g):
         for h in range(2):
             mine, other = along[h]
-            wait_bytes(G.at[core, g, h, mine, pl.ds(0, 3)], recv.at[A1 + 2 * g + h])
+            wait_bytes(G.at[core, g, h, mine, pl.ds(1, 3)], recv.at[A1 + 2 * g + h])
             for d in (2, 1, 3):
-                block = G.at[core, g, h, mine]
+                block = G.at[core, g, h, mine, pl.ds(1, 3)]
                 remote(
                     block, block, A2 + 6 * g + 3 * h, A2 + 6 * g + 3 * h + d - 1,
                     rep, first_peer(h, (mine + d) % 4),
@@ -290,30 +300,61 @@
 
     gather_second(0)
     gather_second(1)
+
+    @pl.when(owner)
+    def _():
+        for k in range(1, 4):
+            block = D.at[core]
+            remote(block, block, SD, SD, ((zl + k) % ZL) * 2 + core, fsdp).start()
+
     gather_first(0)
 
-    @pl.when(zl < OWN)
-    def _():
-        wait_bytes(D.at[core, pl.ds(0, 2)], recv.at[SD])
-
-    @pl.when(zl >= OWN)
+    gather_first(1)
+    share(0)
+
+    @pl.when(jnp.logical_not(owner))
     def _():
         wait_bytes(D.at[core], recv.at[SD])
 
     remote(D.at[core], D.at[core], SDS, SDS, sibling, fsdp).start()
 
-    gather_first(1)
-    share(0)
+    def write(g, h):
+        zh_ = SHARD[g][h]
+        wait_bytes(G.at[1 - core, g, h], recv.at[SC + 2 * g + h])
+        for x_ in range(NX):
+            gu_tiles = []
+            for y_ in range(NY):
+                e1, e2 = (x_, (y_ + 4 - y) % 4) if h == 0 else (y_, (x_ + 4 - x) % 4)
+                col = ((zh_ * NX + x_) * NY + y_) * LANES
+                wide = []
+                for c in range(2):
+                    for k in range(2):
+                        row = 32 * c + 16 * k
+                        dn_out[row : row + 16, col : col + LANES] = G[c, g, h, e1, e2, 16 * k : 16 * k + 16]
+                    tile = G[c, g, h, e1, e2, 32:48].astype(F32)
+                    wide += [tile[0:8], tile[8:16]]
+                gu_tiles.append(wide)
+            for yp in range(NY // 2):
+                even, odd = gu_tiles[2 * yp], gu_tiles[2 * yp + 1]
+                odd = pltpu.roll(jnp.concatenate(odd, axis=1), HALF, 1)
+                joined = jnp.where(lane8 < HALF, even[3], odd[:, 0:128])
+                full = jnp.concatenate(even[:3] + [joined, odd[:, 128:512]], axis=1)
+                col = ((zh_ * NX + x_) * NY + 2 * yp) * GUCOLS
+                for j in range(2):
+                    gu_out[j, :, col : col + 2 * GUCOLS] = full[4 * j : 4 * j + 4].astype(BF)
+
+    write(0, 0)
+    write(0, 1)
+    share(1)
 
     wait_bytes(D.at[1 - core], recv.at[SDS])
-    state = ([], [], [])
+    moments, masters, scales = [], [], []
     for c in range(2):
-        for k in range(OWN):
-            moment = 0.9 * MO[c, k] + D[c, k, 0]
-            state[0].append(moment)
-            state[1].append(M[c, k] - 0.7 * (D[c, k, 0] + 0.9 * moment))
-            state[2].append(D[c, k, 1])
-    moments, masters, scales = ([s[0:3], s[3:6]] for s in state)
+        delta, scale = D[c, 0], D[c, 1]
+        moment = 0.9 * MO[c] + delta
+        master = M[c] - 0.7 * (delta + 0.9 * moment)
+        for tiles, value in ((moments, moment), (masters, master), (scales, scale)):
+            tiles.append([value[16 * k : 16 * k + 16] for k in range(OWN)])
     for tiles, d_out, g_out in ((moments, dmo_out, gmo_out), (masters, dm_out, gm_out)):
         for c in range(2):
             for k in range(2):
@@ -336,55 +377,27 @@
     for j in range(2):
         gs_out[j, :, :] = acc[4 * j : 4 * j + 4, 0:7]
 
-    def write(g, h):
-        zh_ = 2 * h + g
-        wait_bytes(G.at[1 - core, g, h], recv.at[SC + 2 * g + h])
-        for x_ in range(NX):
-            gu_tiles = []
-            for y_ in range(NY):
-                e1, e2 = (x_, y_) if h == 0 else (y_, x_)
-                col = ((zh_ * NX + x_) * NY + y_) * LANES
-                wide = []
-                for c in range(2):
-                    for k in range(2):
-                        row = 32 * c + 16 * k
-                        dn_out[row : row + 16, col : col + LANES] = G[c, g, h, e1, e2, k]
-                    tile = G[c, g, h, e1, e2, 2].astype(F32)
-                    wide += [tile[0:8], tile[8:16]]
-                gu_tiles.append(wide)
-            for yp in range(NY // 2):
-                even, odd = gu_tiles[2 * yp], gu_tiles[2 * yp + 1]
-                odd = pltpu.roll(jnp.concatenate(odd, axis=1), HALF, 1)
-                joined = jnp.where(lane8 < HALF, even[3], odd[:, 0:128])
-                full = jnp.concatenate(even[:3] + [joined, odd[:, 128:512]], axis=1)
-                col = ((zh_ * NX + x_) * NY + 2 * yp) * GUCOLS
-                for j in range(2):
-                    gu_out[j, :, col : col + 2 * GUCOLS] = full[4 * j : 4 * j + 4].astype(BF)
-
-    write(0, 0)
-    write(0, 1)
-    share(1)
     write(1, 0)
     write(1, 1)
 
     for g, h in pairs:
         i = 2 * g + h
         wait_bytes(S.at[g, h, pl.ds(0, 3)], send.at[P1B + i])
-        wait_bytes(R2.at[g, h, pl.ds(0, 7)], send.at[P2 + i])
-        wait_bytes(G.at[core, g, h, 0, pl.ds(0, 3)], send.at[A1 + i])
-        wait_bytes(G.at[core, g, h, pl.ds(0, 3)], send.at[A2 + 3 * i])
+        wait_bytes(R2.at[g, h], send.at[P2 + i])
+        wait_bytes(R3.at[pl.ds(0, 6)], send.at[A1 + i])
+        wait_bytes(R3.at[pl.ds(0, 9)], send.at[A2 + 3 * i])
         wait_bytes(G.at[core, g, h], send.at[SC + i])
     wait_bytes(D.at[core], send.at[SDS])
 
-    @pl.when(zl < OWN)
+    @pl.when(owner)
     def _():
-        wait_bytes(R3.at[pl.ds(0, 22)], send.at[Z3])
+        wait_bytes(R3.at[pl.ds(0, 7)], send.at[Z3])
         wait_bytes(R3.at[pl.ds(0, 15)], send.at[Z0])
-        wait_bytes(D.at[core], send.at[SD])
-
-    @pl.when(zl >= OWN)
+        wait_bytes(R3.at[pl.ds(0, 12)], send.at[SD])
+
+    @pl.when(jnp.logical_not(owner))
     def _():
-        wait_bytes(R3.at[pl.ds(0, 24)], send.at[Z3])
+        wait_bytes(R3.at[pl.ds(0, 8)], send.at[Z3])
 
 
 def place(*refs):
@@ -429,17 +442,17 @@
             pltpu.VMEM((2, 2, 2, 2, 2, 48, LANES), BF),
             pltpu.VMEM((2, 2, 2, 4, 2, 48, LANES), BF),
             pltpu.VMEM((2, 2, 4, 2, 48, LANES), BF),
-            pltpu.VMEM((2, 2, 8, 48, LANES), BF),
-            pltpu.VMEM((4, OWN, 2, 16, LANES), BF),
-            pltpu.VMEM((32, 16, LANES), BF),
-            pltpu.VMEM((2, OWN, 2, 16, LANES), F32),
-            pltpu.VMEM((2, 2, 2, 4, 4, OWN, 16, LANES), BF),
-            pltpu.VMEM((2, OWN, 16, LANES), F32),
-            pltpu.VMEM((2, OWN, 16, LANES), F32),
+            pltpu.VMEM((2, 2, 3, 2, 48, LANES), BF),
+            pltpu.VMEM((4, 2, 48, LANES), BF),
+            pltpu.VMEM((32, 48, LANES), BF),
+            pltpu.VMEM((2, 2, 48, LANES), F32),
+            pltpu.VMEM((2, 2, 2, 4, 4, 48, LANES), BF),
+            pltpu.VMEM((2, 48, LANES), F32),
+            pltpu.VMEM((2, 48, LANES), F32),
             pltpu.SemaphoreType.DMA((NSEM,)),
             pltpu.SemaphoreType.DMA((NSEM,)),
             pltpu.SemaphoreType.DMA((6,)),
-            pltpu.SemaphoreType.REGULAR((3,)),
+            pltpu.SemaphoreType.REGULAR((4,)),
         ],
         compiler_params=pltpu.CompilerParams(
             collective_id=0, has_side_effects=True, vmem_limit_bytes=40 * MIB

time: 55.5 us -> 53.3 us (0.960)
  Pallas kernels: 54.7 us -> 52.5 us
    pallas_call x1, Pallas kernels: 53.5 us -> 51.3 us  [per_device(): pl.pallas_call(kernel, out_shape=shapes, in_specs=[hbm] * 6, out_specs=[v...]
where the time goes in v4:
time: 53.3 us; the launch traced here: 53.1 us
  Pallas kernels  52.5 us (98%)
  between operations  0.64 us (1%)
    pallas_call x1, Pallas kernels, per_device(): pl.pallas_call(kernel, out_shape=shapes, in_specs=[hbm] * 6, out_specs=[v...  51.3 us
    pallas_call x1, Pallas kernels, per_device(): pl.pallas_call(place, out_shape=shapes, in_specs=[vmem] * 8, out_specs=[h...  1.21 us

profile of v4, /device:TPU:1, one launch (start us, length us, event | category | flops | bytes accessed | tf_op | source)
XLA Modules:
  0.0 53.1 jit_solution(4943488187169190930)
XLA Ops:
  0.6 51.3 %shard_map.125 = (bf16[2,4,28672]{2,1,0:T(4,128)(2,1)S(1)}, bf16[64,8192]{1,0:T(8,128)(2,1)S(1)}, f32[2,4,448]{2,1,0:T(4,128)S(1)}, f32[64,128]{1,0:T(8,128)S(1)...) custom-call(bf16[1,1,2,4,28672]{4,3,2,1,0:T(4,128)(2,1)} %gu_ref.1, ...), custom_call_target="tpu_custom_call" | custom-call | tf_op jit(solution)/shard_map/pallas_call | solution.py:429
  51.9 1.2 %shard_map.126 = (bf16[2,4,28672]{2,1,0:T(4,128)(2,1)}, bf16[64,8192]{1,0:T(8,128)(2,1)}, f32[2,4,448]{2,1,0:T(4,128)}, f32[64,128]{1,0:T(8,128)}, f32[2,4,448]{...) custom-call(bf16[2,4,28672]{2,1,0:T(4,128)(2,1)S(1)} %get-tuple-element.24.refs_0_, ...), custom_call_target="tpu_custom_call" | custom-call | tf_op jit(solution)/shard_map/pallas_call | solution.py:461

commit v5 on v4

--- a/solution.py
+++ b/solution.py
@@ -14,7 +14,7 @@
 GUCOLS = 448
 OWN = 3
 SHARD = ((0, 2), (1, 3))
-OWNER = (0, 2)
+OWNER = (2, 0)
 BF = jnp.bfloat16
 F32 = jnp.float32
 MIB = 1024 * 1024
@@ -189,9 +189,9 @@
     ahead(0)
     arrange(1)
     ahead(1)
+    tell(0)
     rest_of(0)
     rest_of(1)
-    tell(0)
     hear(0)
     tell(1)
     pass_on(0)

time: 53.3 us -> 52.3 us (0.981)
  Pallas kernels: 52.5 us -> 51.5 us
    pallas_call x1, Pallas kernels: 51.3 us -> 50.3 us  [per_device(): pl.pallas_call(kernel, out_shape=shapes, in_specs=[hbm] * 6, out_specs=[v...]
where the time goes in v5:
time: 52.3 us; the launch traced here: 52.2 us
  Pallas kernels  51.5 us (98%)
  between operations  0.64 us (1%)
    pallas_call x1, Pallas kernels, per_device(): pl.pallas_call(kernel, out_shape=shapes, in_specs=[hbm] * 6, out_specs=[v...  50.3 us
    pallas_call x1, Pallas kernels, per_device(): pl.pallas_call(place, out_shape=shapes, in_specs=[vmem] * 8, out_specs=[h...  1.21 us

profile of v5, /device:TPU:1, one launch (start us, length us, event | category | flops | bytes accessed | tf_op | source)
XLA Modules:
  0.0 52.2 jit_solution(343892782583601027)
XLA Ops:
  0.6 50.3 %shard_map.125 = (bf16[2,4,28672]{2,1,0:T(4,128)(2,1)S(1)}, bf16[64,8192]{1,0:T(8,128)(2,1)S(1)}, f32[2,4,448]{2,1,0:T(4,128)S(1)}, f32[64,128]{1,0:T(8,128)S(1)...) custom-call(bf16[1,1,2,4,28672]{4,3,2,1,0:T(4,128)(2,1)} %gu_ref.1, ...), custom_call_target="tpu_custom_call" | custom-call | tf_op jit(solution)/shard_map/pallas_call | solution.py:429
  51.0 1.2 %shard_map.126 = (bf16[2,4,28672]{2,1,0:T(4,128)(2,1)}, bf16[64,8192]{1,0:T(8,128)(2,1)}, f32[2,4,448]{2,1,0:T(4,128)}, f32[64,128]{1,0:T(8,128)}, f32[2,4,448]{...) custom-call(bf16[2,4,28672]{2,1,0:T(4,128)(2,1)S(1)} %get-tuple-element.24.refs_0_, ...), custom_call_target="tpu_custom_call" | custom-call | tf_op jit(solution)/shard_map/pallas_call | solution.py:461

commit v6 on v5

--- a/solution.py
+++ b/solution.py
@@ -345,6 +345,22 @@
 
     write(0, 0)
     write(0, 1)
+    for g, h in pairs:
+        i = 2 * g + h
+        wait_bytes(S.at[g, h, pl.ds(0, 3)], send.at[P1B + i])
+        wait_bytes(R2.at[g, h], send.at[P2 + i])
+        wait_bytes(R3.at[pl.ds(0, 6)], send.at[A1 + i])
+
+    @pl.when(owner)
+    def _():
+        wait_bytes(R3.at[pl.ds(0, 7)], send.at[Z3])
+        wait_bytes(R3.at[pl.ds(0, 15)], send.at[Z0])
+        wait_bytes(R3.at[pl.ds(0, 12)], send.at[SD])
+
+    @pl.when(jnp.logical_not(owner))
+    def _():
+        wait_bytes(R3.at[pl.ds(0, 8)], send.at[Z3])
+
     share(1)
 
     wait_bytes(D.at[1 - core], recv.at[SDS])
@@ -382,22 +398,9 @@
 
     for g, h in pairs:
         i = 2 * g + h
-        wait_bytes(S.at[g, h, pl.ds(0, 3)], send.at[P1B + i])
-        wait_bytes(R2.at[g, h], send.at[P2 + i])
-        wait_bytes(R3.at[pl.ds(0, 6)], send.at[A1 + i])
         wait_bytes(R3.at[pl.ds(0, 9)], send.at[A2 + 3 * i])
         wait_bytes(G.at[core, g, h], send.at[SC + i])
     wait_bytes(D.at[core], send.at[SDS])
-
-    @pl.when(owner)
-    def _():
-        wait_bytes(R3.at[pl.ds(0, 7)], send.at[Z3])
-        wait_bytes(R3.at[pl.ds(0, 15)], send.at[Z0])
-        wait_bytes(R3.at[pl.ds(0, 12)], send.at[SD])
-
-    @pl.when(jnp.logical_not(owner))
-    def _():
-        wait_bytes(R3.at[pl.ds(0, 8)], send.at[Z3])
 
 
 def place(*refs):

time: 52.3 us -> 52.3 us (level)
  no operation moved by 1% of the time
where the time goes in v6:
time: 52.3 us; the launch traced here: 52.2 us
  Pallas kernels  51.5 us (98%)
  between operations  0.64 us (1%)
    pallas_call x1, Pallas kernels, per_device(): pl.pallas_call(kernel, out_shape=shapes, in_specs=[hbm] * 6, out_specs=[v...  50.3 us
    pallas_call x1, Pallas kernels, per_device(): pl.pallas_call(place, out_shape=shapes, in_specs=[vmem] * 8, out_specs=[h...  1.21 us

profile of v6, /device:TPU:1, one launch (start us, length us, event | category | flops | bytes accessed | tf_op | source)
XLA Modules:
  0.0 52.2 jit_solution(16320752082083579506)
XLA Ops:
  0.6 50.3 %shard_map.125 = (bf16[2,4,28672]{2,1,0:T(4,128)(2,1)S(1)}, bf16[64,8192]{1,0:T(8,128)(2,1)S(1)}, f32[2,4,448]{2,1,0:T(4,128)S(1)}, f32[64,128]{1,0:T(8,128)S(1)...) custom-call(bf16[1,1,2,4,28672]{4,3,2,1,0:T(4,128)(2,1)} %gu_ref.1, ...), custom_call_target="tpu_custom_call" | custom-call | tf_op jit(solution)/shard_map/pallas_call | solution.py:432
  51.0 1.2 %shard_map.126 = (bf16[2,4,28672]{2,1,0:T(4,128)(2,1)}, bf16[64,8192]{1,0:T(8,128)(2,1)}, f32[2,4,448]{2,1,0:T(4,128)}, f32[64,128]{1,0:T(8,128)}, f32[2,4,448]{...) custom-call(bf16[2,4,28672]{2,1,0:T(4,128)(2,1)S(1)} %get-tuple-element.24.refs_0_, ...), custom_call_target="tpu_custom_call" | custom-call | tf_op jit(solution)/shard_map/pallas_call | solution.py:464
